TPU v7x, 512 devices: a whole 4x8x8 slice. The times are simulated.
512 devices in a mesh: tile: 128 (over y, z, core), pair: 4 (over x).
Axes of the slice: x: 4, y: 8, z: 8, core: 2. Of those that a mesh axis runs over, the one named last changes fastest.
Arguments:
- amplitudes: bfloat16 [48, 512, 800], P(None, ('tile', 'pair')), may hold values from -6 to 6
- integrals: bfloat16 [768, 200, 1600], P('tile', None, 'pair'), may hold values from -0.1875 to 0.1875
- tile_column: int32 [768], P('tile'), may hold values from 0 to 47
- block_symmetry: int32 [128], P('tile'), may hold values from 0 to 3
Outputs:
- residual: bfloat16 [512, 128, 1600], P(('tile', 'pair'))
All inputs are finite; a program needn't handle non-finite values.
Results may differ from a plain program's by a relative error of at most 0.001.
Values may be sent and summed in bfloat16 or wider, within the bound.
No kernel may reach another device: no remote copies, remote signals or barrier semaphores. Data moves between devices by JAX's collectives and lax.ppermute only.
A program may use at most 64 MiB of HBM per device.

v0:
```python
import jax
import jax.numpy as jnp
from jax import lax
from jax.sharding import PartitionSpec as P


def contract_with(amps, tiles):
    tile_count = amps.shape[0]
    lead = amps.shape[1]
    rows = amps.shape[2]
    summed = jnp.zeros((lead * rows, tiles.shape[2]), jnp.float32)
    for slot in range(tile_count):
        flat = amps[slot].reshape(lead * rows, amps.shape[3])
        summed = summed + jnp.dot(flat, tiles[slot], preferred_element_type=jnp.float32)
    return summed.reshape(lead, rows, tiles.shape[2])


def local(amplitudes, integrals, tile_column, block_symmetry):
    owners = lax.axis_size("tile")
    window = amplitudes.shape[0]
    pair_rows = amplitudes.shape[1]
    virtuals = amplitudes.shape[2]
    irrep_width = virtuals // 4
    tile_count = integrals.shape[0]
    columns_all, symmetry_all = (
        lax.all_gather(tile_column, "tile", axis=0, tiled=True),
        lax.all_gather(block_symmetry, "tile", axis=0, tiled=True),
    )
    column_grid = columns_all.reshape(owners, tile_count).T
    wanted_grid = jnp.bitwise_xor(symmetry_all[None, :], column_grid // (window // 4))
    quarters = amplitudes.reshape(window, pair_rows, 4, irrep_width)
    outgoing = quarters[column_grid, :, wanted_grid, :]
    arrived = lax.all_to_all(outgoing, "tile", split_axis=1, concat_axis=1, tiled=True)
    partial_sum = contract_with(arrived, lax.all_gather(integrals, "pair", axis=2, tiled=True))
    outgoing_rows = partial_sum.astype(jnp.bfloat16)
    return lax.all_to_all(outgoing_rows, "tile", split_axis=0, concat_axis=1, tiled=True)


def solution(mesh):
    in_specs = (P(None, ("tile", "pair"), None), P("tile", None, "pair"), P("tile"), P("tile"))
    out_specs = P(("tile", "pair"), None, None)
    return jax.shard_map(local, mesh=mesh, in_specs=in_specs, out_specs=out_specs, check_vma=False)
```

profile of v0, /device:TPU:1, one launch (start us, length us, event | category | flops | bytes accessed | tf_op | source)
XLA Modules:
  0.0 190.2 jit_solution(7423367479008004849)
XLA Ops:
  6.5 4.2 %copy.14 = bf16[6,200,400]{1,0,2:T(8,128)(2,1)} copy(bf16[6,200,400]{2,1,0:T(8,128)(2,1)} %param.5) | data formatting | bytes 1920000 | tf_op args[1]
  11.6 1.3 dynamic-slice
  13.8 0.8 dynamic-update-slice.1
  14.6 28.2 %all-reduce.2 = (s32[768]{0:T(1024)S(1)}, s32[128]{0:T(128)S(1)}) all-reduce(s32[768]{0:T(1024)S(1)} %dynamic-update-slice, s32[128]{0:T(128)S(1)} %dynamic-update-slice.1), channel_id=1, replica_groups=mesh['tile'=128,'pair'=4] {'tile'}, use_global_device_ids=true, to_apply=%add | all-reduce | flops 896 | bytes 7168
  43.0 4.4 %gather_fusion = bf16[768,200]{1,0:T(8,128)(2,1)S(1)} fusion(bf16[48,4,200]{2,1,0:T(4,128)(2,1)S(1)} %reshape.14, s32[768]{0:T(1024)S(1)} %bitcast.62), kind=kCustom, calls=%fused_computation | custom fusion | bytes 620544 | tf_op jit(solution)/shard_map/gather | solution.py:32
  47.7 30.5 %all_to_all.17 = bf16[6,128,1,200]{3,0,2,1:T(8,128)(2,1)S(1)} all-to-all(bf16[6,128,1,200]{3,0,2,1:T(8,128)(2,1)S(1)} %copy.12), channel_id=1, replica_groups=mesh['tile'=128,'pair'=4] {'tile'}, dimensions={1} | all-to-all | bytes 614400 | tf_op jit(solution)/shard_map/all_to_all | solution.py:33
  78.2 0.6 fusion.25
  78.8 0.7 copy.28
  80.2 9.4 %all-gather.2.cloned.1.call-done = bf16[6,200,1600]{1,0,2:T(8,128)(2,1)} async-done(((bf16[6,200,400]{1,0,2:T(8,128)(2,1)}), bf16[6,200,1600]{1,0,2:T(8,128)(2,1)}) %all-gather.2.cloned.1.call-update) | async-done | bytes 3840016 | tf_op jit(solution)/shard_map/all_gather | solution.py:34
  89.6 25.1 %fusion.24 = (bf16[1,200,1600]{1,0,2:T(2,128)(2,1)S(1)}, bf16[1,200,1600]{1,0,2:T(2,128)(2,1)S(1)}, bf16[1,200,1600]{1,0,2:T(2,128)(2,1)}, bf16[1,200,1600]{1,0,...) fusion(bf16[6,200,1600]{1,0,2:T(8,128)(2,1)} %all-gather.2.cloned.1.call-done), kind=kLoop, calls=%fused_computation.36 | loop fusion | bytes 7680000 | tf_op jit(solution)/shard_map/slice | solution.py:14
  114.7 4.8 %copy.29 = bf16[1,200,1600]{2,1,0:T(8,128)(2,1)} copy(bf16[1,200,1600]{1,0,2:T(2,128)(2,1)} %get-tuple-element.12) | data formatting | bytes 1280000
  119.5 4.8 %copy.31 = bf16[1,200,1600]{2,1,0:T(8,128)(2,1)} copy(bf16[1,200,1600]{1,0,2:T(2,128)(2,1)} %get-tuple-element.11) | data formatting | bytes 1280000
  124.3 4.7 %copy.33 = bf16[1,200,1600]{2,1,0:T(8,128)(2,1)} copy(bf16[1,200,1600]{1,0,2:T(2,128)(2,1)} %get-tuple-element.10) | data formatting | bytes 1280000
  129.0 4.7 %copy.35 = bf16[1,200,1600]{2,1,0:T(8,128)(2,1)} copy(bf16[1,200,1600]{1,0,2:T(2,128)(2,1)} %get-tuple-element.9) | data formatting | bytes 1280000
  133.7 3.8 %copy.37 = bf16[1,200,1600]{2,1,0:T(8,128)(2,1)} copy(bf16[1,200,1600]{1,0,2:T(2,128)(2,1)S(1)} %get-tuple-element.8) | data formatting | bytes 1280000
  137.6 3.9 %copy.39 = bf16[1,200,1600]{2,1,0:T(8,128)(2,1)} copy(bf16[1,200,1600]{1,0,2:T(2,128)(2,1)S(1)} %get-tuple-element.7) | data formatting | bytes 1280000
  141.4 0.5 fusion.7
  141.9 0.5 convolution_add_fusion.4
  142.5 0.5 convolution_add_fusion.3
  143.0 0.6 copy-done.2
  143.6 0.5 convolution_add_fusion.2
  144.1 0.6 copy-done.1
  144.7 0.5 convolution_add_fusion.1
  145.2 0.6 copy-done.5
  145.8 0.5 fusion.1
  146.3 0.5 broadcast.36
  146.8 0.9 reduce
  147.7 0.3 copy.40
  148.0 0.5 reshape.48
  148.4 32.4 %all_to_all.18 = bf16[128,2,800]{2,1,0:T(2,128)(2,1)S(1)} all-to-all(bf16[128,2,800]{2,1,0:T(2,128)(2,1)S(1)} %reshape.48), channel_id=1, replica_groups=mesh['tile'=128,'pair'=4] {'tile'}, dimensions={0} | all-to-all | bytes 819200 | tf_op jit(solution)/shard_map/all_to_all | solution.py:36
  180.8 0.6 reshape.49
  181.5 1.8 copy.27
  (30 shorter events, 1.8 us)
Async XLA Ops:
  6.5 4.3 %copy-start.7 = (bf16[48,1,800]{2,0,1:T(8,128)(2,1)S(1)}, bf16[48,1,800]{2,0,1:T(8,128)(2,1)}, u32[]{:S(2)}) copy-start(bf16[48,1,800]{2,0,1:T(8,128)(2,1)} %param.4) | copy-start | bytes 230404
  6.5 83.1 %all-gather.2.cloned.1.call-start = ((), (), s32[]{:S(2)}) async-start(), calls=%async_computation.2 | async-start | bytes 8192000 | tf_op jit(solution)/shard_map/all_gather | solution.py:34
  10.8 2.8 %copy-start.8 = (s32[6]{0:T(128)S(1)}, s32[6]{0:T(128)}, u32[]{:S(2)}) copy-start(s32[6]{0:T(128)} %param.6) | copy-start | bytes 76
  137.6 3.9 %copy-start = (bf16[1,200,1600]{2,1,0:T(8,128)(2,1)S(1)}, bf16[1,200,1600]{2,1,0:T(8,128)(2,1)}, u32[]{:S(2)}) copy-start(bf16[1,200,1600]{2,1,0:T(8,128)(2,1)} %copy.29) | copy-start | bytes 1920004
  137.6 3.9 %copy-start.6 = (bf16[1,128,1,200]{1,3,2,0:T(8,128)(2,1)S(1)}, bf16[1,128,1,200]{1,3,2,0:T(8,128)(2,1)}, u32[]{:S(2)}) copy-start(bf16[1,128,1,200]{1,3,2,0:T(8,128)(2,1)} %copy.28) | copy-start | bytes 153604
  137.6 4.3 %copy-start.4 = (bf16[1,200,1600]{2,1,0:T(8,128)(2,1)S(1)}, bf16[1,200,1600]{2,1,0:T(8,128)(2,1)}, u32[]{:S(2)}) copy-start(bf16[1,200,1600]{2,1,0:T(8,128)(2,1)} %copy.31) | copy-start | bytes 1920004
  141.4 1.1 copy-start.3
  142.5 1.1 copy-start.2
  143.6 1.1 copy-start.1
  144.7 1.1 copy-start.5
Sparse Core Ops, SparseCore 0:
  10.9 78.6 all-gather.1
where the time goes:
time: 191 us; the launch traced here: 190 us
  blocking collectives  91.1 us (48%)
  local copies, waits for them, and re-layouts  71 us (37%)
  between operations  14.9 us (8%)
  waiting for transfers between devices  9.39 us (5%)
  matrix products  2.81 us (1%)
    unnamed x39, local copies, waits for them, and re-layouts  38 us
    all_to_all x1, blocking collectives, local(): lax.all_to_all(outgoing_rows, 'tile', split_axis=0, concat_axis=1, tiled=...  32.4 us
    all_to_all x1, blocking collectives, local(): lax.all_to_all(outgoing, 'tile', split_axis=1, concat_axis=1, tiled=True)  30.5 us
    unnamed x1, blocking collectives  28.2 us
    slice x1, local copies, waits for them, and re-layouts, contract_with(): tiles[slot]  25.1 us
    all_gather x1, waiting for transfers between devices, local(): lax.all_gather(integrals, 'pair', axis=2, tiled=True)  9.37 us
    gather x2, local copies, waits for them, and re-layouts, local(): outgoing = quarters[column_grid, :, wanted_grid, :]  4.62 us
  transfers between devices with their start and end apart: 1, of which 1 were waited for; matrix products, arithmetic and copies ran while one was open for 5% of the time, Pallas kernels for 0%

commit v1 on v0

v1 whole, which is shorter than its diff:
```python
import functools

import jax
import jax.numpy as jnp
from jax import lax
from jax.experimental import pallas as pl
from jax.experimental.pallas import tpu as pltpu
from jax.sharding import Mesh, PartitionSpec as P

LANES = 128
BF16 = jnp.bfloat16
F32 = jnp.float32

HEAD = 128
MIDDLE = 64
LAST = 8


def pack_kernel(w_ref, out_ref):
    slots, width, columns = w_ref.shape
    depth = slots * width
    slabs = columns // LANES
    left = columns - slabs * LANES

    def ordered(lo, hi):
        heads = [w_ref[k, :HEAD, lo:hi] for k in range(slots)]
        middles = [w_ref[k, HEAD : HEAD + MIDDLE, lo:hi] for k in range(slots)]
        ends = [w_ref[k, HEAD + MIDDLE :, lo:hi].astype(F32) for k in range(slots)]
        return heads + middles + [jnp.concatenate(ends, axis=0).astype(BF16)]

    for s in range(slabs):
        at = s * depth
        for part in ordered(s * LANES, (s + 1) * LANES):
            out_ref[at : at + part.shape[0], :] = part
            at += part.shape[0]
    narrow = jnp.concatenate(ordered(slabs * LANES, columns), axis=0)
    eye = (
        lax.broadcasted_iota(jnp.int32, (left, left), 0) == lax.broadcasted_iota(jnp.int32, (left, left), 1)
    ).astype(BF16)
    turned = lax.dot_general(eye, narrow, (((1,), (1,)), ((), ())), preferred_element_type=F32)
    chunks = -(-depth // LANES)
    turned = jnp.concatenate([turned, jnp.zeros((left, chunks * LANES - depth), F32)], axis=1).astype(BF16)
    for j in range(chunks):
        at = slabs * depth + j * left
        out_ref[at : at + left, :] = turned[:, j * LANES : (j + 1) * LANES]


def pack(integrals):
    slots, width, columns = integrals.shape
    slabs = columns // LANES
    left = columns - slabs * LANES
    rows = slabs * slots * width + -(-slots * width // LANES) * left
    return pl.pallas_call(
        pack_kernel,
        out_shape=jax.ShapeDtypeStruct((rows, LANES), BF16),
        in_specs=[pl.BlockSpec(memory_space=pltpu.VMEM)],
        out_specs=pl.BlockSpec(memory_space=pltpu.VMEM),
        compiler_params=pltpu.CompilerParams(vmem_limit_bytes=24 << 20),
        cost_estimate=pl.CostEstimate(flops=0, bytes_accessed=4 * rows * LANES, transcendentals=0),
        name="pack_integrals",
    )(integrals)


def select_kernel(slots, core_ref, own_ref, other_ref, wanted_ref, out_ref):
    window, virtuals = own_ref.shape
    width = virtuals // 4
    peers = wanted_ref.shape[0]
    first = core_ref[0] == 0
    own = own_ref[...].astype(F32)
    other = other_ref[...].astype(F32)
    rows = [jnp.where(first, own, other), jnp.where(first, other, own)]
    blank = jnp.zeros((4 * window, 2 * LANES - width), F32)
    quarters = [jnp.concatenate([row[:, h * width : (h + 1) * width] for h in range(4)], axis=0) for row in rows]
    table = jnp.concatenate([quarters[0], blank, quarters[1], blank], axis=1).astype(BF16)
    places = lax.broadcasted_iota(jnp.int32, (peers, 4 * window), 1)
    wanted = wanted_ref[...]
    pieces = []
    for k in range(slots):
        chosen = (places == wanted[:, k : k + 1]).astype(F32).astype(BF16)
        pieces.append(jnp.dot(chosen, table, preferred_element_type=F32))
    chunks = out_ref.shape[0] // 2
    for r in range(2):
        base = r * 2 * LANES
        for k in range(slots):
            out_ref[r * chunks + k] = pieces[k][:, base : base + LANES].astype(BF16)
        for j in range(slots // 2):
            lo, hi = base + HEAD, base + HEAD + MIDDLE
            pair = [pieces[2 * j][:, lo:hi], pieces[2 * j + 1][:, lo:hi]]
            out_ref[r * chunks + slots + j] = jnp.concatenate(pair, axis=1).astype(BF16)
        lo = base + HEAD + MIDDLE
        ends = [pieces[k][:, lo : lo + LAST] for k in range(slots)]
        ends.append(jnp.zeros((peers, LANES - slots * LAST), F32))
        out_ref[r * chunks + chunks - 1] = jnp.concatenate(ends, axis=1).astype(BF16)


def select(slots, core, own, other, wanted):
    peers = wanted.shape[0]
    chunks = slots + slots // 2 + 1
    whole = pl.BlockSpec(memory_space=pltpu.VMEM)
    return pl.pallas_call(
        functools.partial(select_kernel, slots),
        out_shape=jax.ShapeDtypeStruct((2 * chunks, peers, LANES), BF16),
        in_specs=[pl.BlockSpec(memory_space=pltpu.SMEM), whole, whole, whole],
        out_specs=whole,
        compiler_params=pltpu.CompilerParams(vmem_limit_bytes=24 << 20),
        name="select_pieces",
    )(core, own, other, wanted)


def contract_kernel(depth, columns, a_ref, w_ref, out_ref, tails):
    p = pl.program_id(0)
    chunks = a_ref.shape[0] // 2
    slabs = columns // LANES
    left = columns - slabs * LANES
    halves = [jnp.concatenate([a_ref[r * chunks + j] for j in range(chunks)], axis=1) for r in range(2)]
    a = jnp.concatenate(halves, axis=0)
    w = jnp.concatenate([w_ref[0, s * depth : (s + 1) * depth, :] for s in range(slabs)], axis=1)
    product = jnp.dot(a[:, :depth], w, preferred_element_type=F32).astype(BF16)
    for s in range(slabs):
        out_ref[slabs * p + s] = product[:, s * LANES : (s + 1) * LANES]
    base = slabs * depth
    parts = [w_ref[0, base + j * left : base + (j + 1) * left, :] for j in range(chunks)]

    @pl.when(p == 0)
    def _():
        tails[...] = jnp.zeros_like(tails)

    tails[pl.ds(pl.multiple_of(p * left, left), left), :] = jnp.concatenate(parts, axis=1)

    @pl.when(p == pl.num_programs(0) - 1)
    def _():
        last = lax.dot_general(a, tails[...], (((1,), (1,)), ((), ())), preferred_element_type=F32)
        out_ref[out_ref.shape[0] - 1] = last.astype(BF16)


def contract(depth, columns, arrived, gathered):
    ring, rows, _ = gathered.shape
    chunks2, peers, _ = arrived.shape
    slabs = columns // LANES
    outs = ring * slabs + 1
    return pl.pallas_call(
        functools.partial(contract_kernel, depth, columns),
        grid=(ring,),
        out_shape=jax.ShapeDtypeStruct((outs, 2 * peers, LANES), BF16),
        in_specs=[
            pl.BlockSpec((chunks2, peers, LANES), lambda p: (0, 0, 0)),
            pl.BlockSpec((1, rows, LANES), lambda p: (p, 0, 0)),
        ],
        out_specs=pl.BlockSpec((outs, 2 * peers, LANES), lambda p: (0, 0, 0)),
        scratch_shapes=[pltpu.VMEM((LANES, chunks2 // 2 * LANES), BF16)],
        compiler_params=pltpu.CompilerParams(vmem_limit_bytes=24 << 20),
        name="contract",
    )(arrived, gathered)


def place_kernel(columns, r_ref, out_ref):
    count, blocks, _ = r_ref.shape
    half = blocks // 2
    slabs = columns // LANES
    left = columns - slabs * LANES
    came = lax.broadcasted_iota(jnp.int32, (blocks, blocks), 0)
    goes = lax.broadcasted_iota(jnp.int32, (blocks, blocks), 1)
    order = jnp.where(came < half, 2 * came, 2 * (came - half) + 1)
    turn = (order == goes).astype(F32).astype(BF16)
    for j in range(count):
        block = lax.dot_general(r_ref[j], turn, (((0,), (0,)), ((), ())), preferred_element_type=F32).astype(BF16)
        if j < count - 1:
            at = j // slabs * columns + j % slabs * LANES
            out_ref[at : at + LANES, :] = block
        else:
            for p in range((count - 1) // slabs):
                at = p * columns + slabs * LANES
                out_ref[at : at + left, :] = block[p * left : (p + 1) * left]


def place(columns, received):
    count, blocks, _ = received.shape
    ring = (count - 1) // (columns // LANES)
    whole = pl.BlockSpec(memory_space=pltpu.VMEM)
    return pl.pallas_call(
        functools.partial(place_kernel, columns),
        out_shape=jax.ShapeDtypeStruct((ring * columns, blocks), BF16),
        in_specs=[whole],
        out_specs=whole,
        compiler_params=pltpu.CompilerParams(vmem_limit_bytes=24 << 20),
        name="place_rows",
    )(received)


def local(amplitudes, integrals, tile_column, block_symmetry):
    window, _, virtuals = amplitudes.shape
    slots, width, columns = integrals.shape
    depth = slots * width
    peers = lax.axis_size("y") * lax.axis_size("z")
    core = lax.axis_index("core")

    packed = pack(integrals)
    gathered = lax.all_gather(packed, "pair", axis=0, tiled=False)

    own = amplitudes.reshape(window, virtuals)
    other = lax.ppermute(own, "core", [(0, 1), (1, 0)])
    symmetry = jnp.bitwise_xor(block_symmetry[0], tile_column // (window // 4))
    wanted = jnp.zeros((LANES,), jnp.int32).at[:slots].set(symmetry * window + tile_column)
    asked = lax.all_to_all(jnp.broadcast_to(wanted, (peers, LANES)), ("y", "z"), 0, 0, tiled=True)

    outgoing = select(slots, core.reshape(1), own, other, asked)
    arrived = lax.all_to_all(outgoing, ("y", "z"), 1, 1, tiled=True)
    rows = contract(depth, columns, arrived, gathered)
    received = lax.all_to_all(rows, ("core", "y", "z"), 1, 1, tiled=True)
    return place(columns, received).T[None]


def solution(mesh):
    sizes = {2: (1, 1), 8: (2, 2), 128: (8, 8)}[mesh.shape["tile"]]
    fine = Mesh(mesh.devices.reshape(*sizes, 2, mesh.shape["pair"]), ("y", "z", "core", "pair"))
    tile = ("y", "z", "core")
    in_specs = (P(None, (*tile, "pair"), None), P(tile, None, "pair"), P(tile), P(tile))
    out_specs = P((*tile, "pair"), None, None)
    return jax.shard_map(local, mesh=fine, in_specs=in_specs, out_specs=out_specs, check_vma=False)
```

time: 191 us -> 114 us (0.60)
  local copies, waits for them, and re-layouts: 71 us -> 5.59 us
  blocking collectives: 91.1 us -> 53.5 us
  starting transfers between devices: 0.01 us -> 19.7 us
  waiting for transfers between devices: 9.39 us -> 15.3 us
  Pallas kernels: 0 us -> 4.42 us
  matrix products: 2.81 us -> 0 us
    unnamed x39 -> x6, local copies, waits for them, and re-layouts: 38 us -> 4.27 us
    unnamed x1 -> x0, blocking collectives: 28.2 us -> none
    slice x2 -> x0, local copies, waits for them, and re-layouts: 25.7 us -> none  [the longest x1 25.1 us: contract_with(): tiles[slot]]
    all_to_all x0 -> x1, starting transfers between devices: none -> 10.9 us  [local(): lax.all_to_all(jnp.broadcast_to(wanted, (peers, LANES)), ('y', 'z'), 0, 0...]
    all_to_all x0 -> x1, waiting for transfers between devices: none -> 10.8 us  [local(): lax.all_to_all(jnp.broadcast_to(wanted, (peers, LANES)), ('y', 'z'), 0, 0...]
    all_to_all x2, blocking collectives: 62.9 us -> 53.5 us  [the longest x1 35.5 us: local(): received = lax.all_to_all(rows, ('core', 'y', 'z'), 1, 1, tiled=True)]
    ppermute x0 -> x1, starting transfers between devices: none -> 8.79 us  [local(): other = lax.ppermute(own, 'core', [(0, 1), (1, 0)])]
    all_gather x1, waiting for transfers between devices: 9.37 us -> 4.51 us  [local(): gathered = lax.all_gather(packed, 'pair', axis=0, tiled=False)]
  transfers between devices with their start and end apart: 1 -> 3, of which waited for: 1 -> 2; matrix products, arithmetic and copies ran while one was open for 5% -> 1% of each run, Pallas kernels for 0% -> 0%
where the time goes in v1:
time: 114 us; the launch traced here: 113 us
  blocking collectives  53.5 us (47%)
  starting transfers between devices  19.7 us (17%)
  waiting for transfers between devices  15.3 us (13%)
  between operations  14.1 us (12%)
  local copies, waits for them, and re-layouts  5.59 us (5%)
  Pallas kernels  4.42 us (4%)
    all_to_all x1, blocking collectives, local(): received = lax.all_to_all(rows, ('core', 'y', 'z'), 1, 1, tiled=True)  35.5 us
    all_to_all x1, blocking collectives, local(): arrived = lax.all_to_all(outgoing, ('y', 'z'), 1, 1, tiled=True)  18 us
    all_to_all x1, starting transfers between devices, local(): lax.all_to_all(jnp.broadcast_to(wanted, (peers, LANES)), ('y', 'z'), 0, 0...  10.9 us
    all_to_all x1, waiting for transfers between devices, local(): lax.all_to_all(jnp.broadcast_to(wanted, (peers, LANES)), ('y', 'z'), 0, 0...  10.8 us
    ppermute x1, starting transfers between devices, local(): other = lax.ppermute(own, 'core', [(0, 1), (1, 0)])  8.79 us
    all_gather x1, waiting for transfers between devices, local(): gathered = lax.all_gather(packed, 'pair', axis=0, tiled=False)  4.51 us
    unnamed x6, local copies, waits for them, and re-layouts  4.27 us
  transfers between devices with their start and end apart: 3, of which 2 were waited for; matrix products, arithmetic and copies ran while one was open for 1% of the time, Pallas kernels for 0%

profile of v1, /device:TPU:1, one launch (start us, length us, event | category | flops | bytes accessed | tf_op | source)
XLA Modules:
  0.0 113.3 jit_solution(12768214004293004790)
XLA Ops:
  6.5 0.0 all-gather.3.cloned.1.call-start
  6.5 0.0 copy-start.1
  6.5 1.3 %copy-done.1 = bf16[6,200,400]{2,1,0:T(8,128)(2,1)S(1)} copy-done((bf16[6,200,400]{2,1,0:T(8,128)(2,1)S(1)}, bf16[6,200,400]{2,1,0:T(8,128)(2,1)}, u32[]{:S(2)}) %copy-start.1) | copy-done | bytes 960024
  7.8 1.2 %pack_integrals.1 = bf16[3760,128]{1,0:T(8,128)(2,1)} custom-call(bf16[6,200,400]{2,1,0:T(8,128)(2,1)S(1)} %copy-done.1), custom_call_target="tpu_custom_call" | custom-call | bytes 1925120 | tf_op jit(solution)/shard_map/pack_integrals/pallas_call | solution.py:53
  9.0 0.0 all-gather.3.cloned.1.call-update
  9.0 8.8 %collective-permute-start = (bf16[48,800]{1,0:T(8,128)(2,1)}, bf16[48,800]{1,0:T(8,128)(2,1)S(1)}, u32[]{:S(2)}, u32[]{:S(2)}) collective-permute-start(bf16[48,800]{1,0:T(8,128)(2,1)} %bitcast.11), channel_id=1, source_target_pairs={{0,4},{4,0},{1,5},{5,1},{2,6},{6,2},{3,7},{7,3},{8,12},{12,8},{9,1... | collective-permute-start | bytes 230408 | tf_op jit(solution)/shard_map/ppermute | solution.py:201
  18.5 0.7 multiply_add_fusion
  19.2 0.6 broadcast_in_dim.7
  19.8 10.9 %all-to-all-start = ((s32[64,1,128]{2,1,0:T(1,128)}), s32[64,1,128]{2,1,0:T(1,128)S(1)}, u32[]{:S(2)}, u32[]{:S(2)}) async-start(s32[64,1,128]{2,1,0:T(1,128)} %broadcast_in_dim.7), calls=%async_computation | async-start | bytes 65536 | tf_op jit(solution)/shard_map/all_to_all | solution.py:204
  30.7 10.8 %all-to-all-done = s32[64,1,128]{2,1,0:T(1,128)S(1)} async-done(((s32[64,1,128]{2,1,0:T(1,128)}), s32[64,1,128]{2,1,0:T(1,128)S(1)}, u32[]{:S(2)}, u32[]{:S(2)}) %all-to-all-start) | async-done | bytes 32800 | tf_op jit(solution)/shard_map/all_to_all | solution.py:204
  41.5 0.0 collective-permute-done.other_ref
  41.5 0.0 copy-start.2
  41.5 0.9 copy-done.2
  42.4 0.5 select_pieces.1
  42.9 0.2 copy.5
  43.2 18.0 %all_to_all.18 = bf16[20,64,128]{2,0,1:T(8,128)(2,1)S(1)} all-to-all(bf16[20,64,128]{2,0,1:T(8,128)(2,1)S(1)} %copy.5), channel_id=1, replica_groups=mesh['y'=8,'z'=8,'core'=2,'pair'=4] {'y','z'}, dimensions={1} | all-to-all | bytes 655360 | tf_op jit(solution)/shard_map/all_to_all | solution.py:207
  61.1 0.1 copy.6.a_ref
  61.2 4.5 %all-gather.3.cloned.1.call-done = bf16[15040,128]{1,0:T(8,128)(2,1)} async-done(((bf16[3760,128]{1,0:T(8,128)(2,1)}), bf16[15040,128]{1,0:T(8,128)(2,1)}) %all-gather.3.cloned.1.call-update) | async-done | bytes 3850256 | tf_op jit(solution)/shard_map/all_gather | solution.py:198
  65.7 0.0 copy-start
  65.7 2.1 %copy-done = bf16[15040,128]{1,0:T(8,128)(2,1)S(1)} copy-done((bf16[15040,128]{1,0:T(8,128)(2,1)S(1)}, bf16[15040,128]{1,0:T(8,128)(2,1)}, u32[]{:S(2)}) %copy-start) | copy-done | bytes 3850264
  67.8 1.7 %contract.1 = bf16[13,128,128]{2,1,0:T(8,128)(2,1)S(1)} custom-call(bf16[20,64,128]{2,1,0:T(8,128)(2,1)S(1)} %copy.6.a_ref, bf16[4,3760,128]{2,1,0:T(8,128)(2,1)S(1)} %bitcast.9), custom_call_target="tpu_custom_call" | custom-call | tf_op jit(solution)/shard_map/contract/pallas_call | solution.py:141
  69.5 0.3 copy.7
  69.8 35.5 %all_to_all.19 = bf16[13,128,128]{2,0,1:T(8,128)(2,1)S(1)} all-to-all(bf16[13,128,128]{2,0,1:T(8,128)(2,1)S(1)} %copy.7), channel_id=1, replica_groups=mesh['y'=8,'z'=8,'core'=2,'pair'=4] {'core','y','z'}, dimensions={1} | all-to-all | bytes 851968 | tf_op jit(solution)/shard_map/all_to_all | solution.py:209
  105.3 0.1 copy.8.r_ref
  105.4 1.1 place_rows.1
  (1 shorter events, 0.0 us)
Async XLA Ops:
  6.5 59.2 %all-gather.3.cloned.1.call-start = ((), (), s32[]{:S(2)}) async-start(), calls=%async_computation.3 | async-start | bytes 4812800 | tf_op jit(solution)/shard_map/all_gather | solution.py:198
  6.5 1.3 %copy-start.1 = (bf16[6,200,400]{2,1,0:T(8,128)(2,1)S(1)}, bf16[6,200,400]{2,1,0:T(8,128)(2,1)}, u32[]{:S(2)}) copy-start(bf16[6,200,400]{2,1,0:T(8,128)(2,1)} %w_ref.1) | copy-start | bytes 2880004
  9.0 32.5 %collective-permute-start = (bf16[48,800]{1,0:T(8,128)(2,1)}, bf16[48,800]{1,0:T(8,128)(2,1)S(1)}, u32[]{:S(2)}, u32[]{:S(2)}) collective-permute-start(bf16[48,800]{1,0:T(8,128)(2,1)} %bitcast.11), channel_id=1, source_target_pairs={{0,4},{4,0},{1,5},{5,1},{2,6},{6,2},{3,7},{7,3},{8,12},{12,8},{9,1... | collective-permute-start | bytes 230408 | tf_op jit(solution)/shard_map/ppermute | solution.py:201
  19.8 21.7 %all-to-all-start = ((s32[64,1,128]{2,1,0:T(1,128)}), s32[64,1,128]{2,1,0:T(1,128)S(1)}, u32[]{:S(2)}, u32[]{:S(2)}) async-start(s32[64,1,128]{2,1,0:T(1,128)} %broadcast_in_dim.7), calls=%async_computation | async-start | bytes 65536 | tf_op jit(solution)/shard_map/all_to_all | solution.py:204
  41.5 0.9 copy-start.2
  65.7 2.1 %copy-start = (bf16[15040,128]{1,0:T(8,128)(2,1)S(1)}, bf16[15040,128]{1,0:T(8,128)(2,1)}, u32[]{:S(2)}) copy-start(bf16[15040,128]{1,0:T(8,128)(2,1)} %all-gather.3.cloned.1.call-done) | copy-start | bytes 11550724
Sparse Core Ops, SparseCore 0:
  9.5 56.2 all-gather.2

commit v2 on v1

--- a/solution.py
+++ b/solution.py
@@ -14,7 +14,6 @@
 HEAD = 128
 MIDDLE = 64
 LAST = 8
-
 
 def pack_kernel(w_ref, out_ref):
     slots, width, columns = w_ref.shape
@@ -49,31 +48,73 @@
     slots, width, columns = integrals.shape
     slabs = columns // LANES
     left = columns - slabs * LANES
-    rows = slabs * slots * width + -(-slots * width // LANES) * left
+    depth = slots * width
+    rows = slabs * depth + -(-depth // LANES) * left
+    whole = pl.BlockSpec(memory_space=pltpu.VMEM)
     return pl.pallas_call(
         pack_kernel,
         out_shape=jax.ShapeDtypeStruct((rows, LANES), BF16),
-        in_specs=[pl.BlockSpec(memory_space=pltpu.VMEM)],
-        out_specs=pl.BlockSpec(memory_space=pltpu.VMEM),
-        compiler_params=pltpu.CompilerParams(vmem_limit_bytes=24 << 20),
-        cost_estimate=pl.CostEstimate(flops=0, bytes_accessed=4 * rows * LANES, transcendentals=0),
+        in_specs=[whole],
+        out_specs=whole,
+        compiler_params=pltpu.CompilerParams(vmem_limit_bytes=24 << 20),
         name="pack_integrals",
     )(integrals)
 
 
-def select_kernel(slots, core_ref, own_ref, other_ref, wanted_ref, out_ref):
+def ask_kernel(window, column_ref, symmetry_ref, out_ref):
+    peers, tile, _ = out_ref.shape
+    lanes = lax.broadcasted_iota(jnp.int32, (tile, LANES), 1)
+    row = jnp.zeros((tile, LANES), F32)
+    for k in range(column_ref.shape[0]):
+        column = column_ref[k]
+        irrep = sum((column >= h * (window // 4)).astype(jnp.int32) for h in (1, 2, 3))
+        place = jnp.bitwise_xor(symmetry_ref[0], irrep) * window + column
+        row = jnp.where(lanes == k, place.astype(F32), row)
+    row = row.astype(BF16)
+    for j in range(peers):
+        out_ref[j] = row
+
+
+def ask(window, peers, tile_column, block_symmetry):
+    scalars = pl.BlockSpec(memory_space=pltpu.SMEM)
+    return pl.pallas_call(
+        functools.partial(ask_kernel, window),
+        out_shape=jax.ShapeDtypeStruct((peers, 8, LANES), BF16),
+        in_specs=[scalars, scalars],
+        out_specs=pl.BlockSpec(memory_space=pltpu.VMEM),
+        name="ask_pieces",
+    )(tile_column, block_symmetry)
+
+
+def table_kernel(core_ref, own_ref, other_ref, out_ref):
     window, virtuals = own_ref.shape
     width = virtuals // 4
-    peers = wanted_ref.shape[0]
     first = core_ref[0] == 0
     own = own_ref[...].astype(F32)
     other = other_ref[...].astype(F32)
     rows = [jnp.where(first, own, other), jnp.where(first, other, own)]
     blank = jnp.zeros((4 * window, 2 * LANES - width), F32)
     quarters = [jnp.concatenate([row[:, h * width : (h + 1) * width] for h in range(4)], axis=0) for row in rows]
-    table = jnp.concatenate([quarters[0], blank, quarters[1], blank], axis=1).astype(BF16)
-    places = lax.broadcasted_iota(jnp.int32, (peers, 4 * window), 1)
-    wanted = wanted_ref[...]
+    out_ref[...] = jnp.concatenate([quarters[0], blank, quarters[1], blank], axis=1).astype(BF16)
+
+
+def build_table(core, own, other):
+    whole = pl.BlockSpec(memory_space=pltpu.VMEM)
+    return pl.pallas_call(
+        table_kernel,
+        out_shape=jax.ShapeDtypeStruct((4 * own.shape[0], 4 * LANES), BF16),
+        in_specs=[pl.BlockSpec(memory_space=pltpu.SMEM), whole, whole],
+        out_specs=whole,
+        compiler_params=pltpu.CompilerParams(vmem_limit_bytes=24 << 20),
+        name="build_table",
+    )(core, own, other)
+
+
+def select_kernel(slots, table_ref, asked_ref, out_ref):
+    peers = asked_ref.shape[0]
+    table = table_ref[...]
+    wanted = asked_ref[...].astype(F32)[:, 0, :].astype(jnp.int32)
+    places = lax.broadcasted_iota(jnp.int32, (peers, table.shape[0]), 1)
     pieces = []
     for k in range(slots):
         chosen = (places == wanted[:, k : k + 1]).astype(F32).astype(BF16)
@@ -93,64 +134,55 @@
         out_ref[r * chunks + chunks - 1] = jnp.concatenate(ends, axis=1).astype(BF16)
 
 
-def select(slots, core, own, other, wanted):
-    peers = wanted.shape[0]
+def select(slots, table, asked):
+    peers = asked.shape[0]
     chunks = slots + slots // 2 + 1
     whole = pl.BlockSpec(memory_space=pltpu.VMEM)
     return pl.pallas_call(
         functools.partial(select_kernel, slots),
         out_shape=jax.ShapeDtypeStruct((2 * chunks, peers, LANES), BF16),
-        in_specs=[pl.BlockSpec(memory_space=pltpu.SMEM), whole, whole, whole],
+        in_specs=[whole, whole],
         out_specs=whole,
         compiler_params=pltpu.CompilerParams(vmem_limit_bytes=24 << 20),
         name="select_pieces",
-    )(core, own, other, wanted)
-
-
-def contract_kernel(depth, columns, a_ref, w_ref, out_ref, tails):
-    p = pl.program_id(0)
+    )(table, asked)
+
+
+def contract_kernel(depth, columns, me_ref, a_ref, *refs):
+    parts, out_ref, tails = refs[:-2], refs[-2], refs[-1]
+    ring = len(parts)
     chunks = a_ref.shape[0] // 2
     slabs = columns // LANES
     left = columns - slabs * LANES
     halves = [jnp.concatenate([a_ref[r * chunks + j] for j in range(chunks)], axis=1) for r in range(2)]
     a = jnp.concatenate(halves, axis=0)
-    w = jnp.concatenate([w_ref[0, s * depth : (s + 1) * depth, :] for s in range(slabs)], axis=1)
-    product = jnp.dot(a[:, :depth], w, preferred_element_type=F32).astype(BF16)
-    for s in range(slabs):
-        out_ref[slabs * p + s] = product[:, s * LANES : (s + 1) * LANES]
-    base = slabs * depth
-    parts = [w_ref[0, base + j * left : base + (j + 1) * left, :] for j in range(chunks)]
-
-    @pl.when(p == 0)
-    def _():
-        tails[...] = jnp.zeros_like(tails)
-
-    tails[pl.ds(pl.multiple_of(p * left, left), left), :] = jnp.concatenate(parts, axis=1)
-
-    @pl.when(p == pl.num_programs(0) - 1)
-    def _():
-        last = lax.dot_general(a, tails[...], (((1,), (1,)), ((), ())), preferred_element_type=F32)
-        out_ref[out_ref.shape[0] - 1] = last.astype(BF16)
-
-
-def contract(depth, columns, arrived, gathered):
-    ring, rows, _ = gathered.shape
+    tails[...] = jnp.zeros_like(tails)
+    for step, part in enumerate(parts):
+        p = lax.rem(me_ref[0] + step, ring)
+        wide = jnp.concatenate([part[s * depth : (s + 1) * depth, :] for s in range(slabs)], axis=1)
+        product = jnp.dot(a[:, :depth], wide, preferred_element_type=F32).astype(BF16)
+        for s in range(slabs):
+            out_ref[slabs * p + s] = product[:, s * LANES : (s + 1) * LANES]
+        narrow = [part[at : at + left, :] for at in range(slabs * depth, part.shape[0], left)]
+        tails[pl.ds(pl.multiple_of(p * left, left), left), :] = jnp.concatenate(narrow, axis=1)
+    last = lax.dot_general(a, tails[...], (((1,), (1,)), ((), ())), preferred_element_type=F32)
+    out_ref[out_ref.shape[0] - 1] = last.astype(BF16)
+
+
+def contract(depth, columns, me, arrived, parts):
+    ring = len(parts)
     chunks2, peers, _ = arrived.shape
-    slabs = columns // LANES
-    outs = ring * slabs + 1
+    outs = ring * (columns // LANES) + 1
+    whole = pl.BlockSpec(memory_space=pltpu.VMEM)
     return pl.pallas_call(
         functools.partial(contract_kernel, depth, columns),
-        grid=(ring,),
         out_shape=jax.ShapeDtypeStruct((outs, 2 * peers, LANES), BF16),
-        in_specs=[
-            pl.BlockSpec((chunks2, peers, LANES), lambda p: (0, 0, 0)),
-            pl.BlockSpec((1, rows, LANES), lambda p: (p, 0, 0)),
-        ],
-        out_specs=pl.BlockSpec((outs, 2 * peers, LANES), lambda p: (0, 0, 0)),
+        in_specs=[pl.BlockSpec(memory_space=pltpu.SMEM)] + [whole] * (1 + ring),
+        out_specs=whole,
         scratch_shapes=[pltpu.VMEM((LANES, chunks2 // 2 * LANES), BF16)],
         compiler_params=pltpu.CompilerParams(vmem_limit_bytes=24 << 20),
         name="contract",
-    )(arrived, gathered)
+    )(me, arrived, *parts)
 
 
 def place_kernel(columns, r_ref, out_ref):
@@ -191,21 +223,21 @@
     window, _, virtuals = amplitudes.shape
     slots, width, columns = integrals.shape
     depth = slots * width
+    ring = lax.axis_size("pair")
     peers = lax.axis_size("y") * lax.axis_size("z")
-    core = lax.axis_index("core")
 
     packed = pack(integrals)
-    gathered = lax.all_gather(packed, "pair", axis=0, tiled=False)
+    asked = lax.all_to_all(ask(window, peers, tile_column, block_symmetry), ("y", "z"), 0, 0, tiled=True)
 
     own = amplitudes.reshape(window, virtuals)
     other = lax.ppermute(own, "core", [(0, 1), (1, 0)])
-    symmetry = jnp.bitwise_xor(block_symmetry[0], tile_column // (window // 4))
-    wanted = jnp.zeros((LANES,), jnp.int32).at[:slots].set(symmetry * window + tile_column)
-    asked = lax.all_to_all(jnp.broadcast_to(wanted, (peers, LANES)), ("y", "z"), 0, 0, tiled=True)
-
-    outgoing = select(slots, core.reshape(1), own, other, asked)
+    table = build_table(lax.axis_index("core").reshape(1), own, other)
+    parts = [packed]
+    parts += [lax.ppermute(packed, "pair", [((i + k) % ring, i) for i in range(ring)]) for k in range(1, ring)]
+
+    outgoing = select(slots, table, asked)
     arrived = lax.all_to_all(outgoing, ("y", "z"), 1, 1, tiled=True)
-    rows = contract(depth, columns, arrived, gathered)
+    rows = contract(depth, columns, lax.axis_index("pair").reshape(1), arrived, parts)
     received = lax.all_to_all(rows, ("core", "y", "z"), 1, 1, tiled=True)
     return place(columns, received).T[None]
 

time: 114 us -> 98.7 us (0.87)
  blocking collectives: 53.5 us -> 30.7 us
  starting transfers between devices: 19.7 us -> 37.1 us
  between operations: 14.1 us -> 0.78 us
  waiting for transfers between devices: 15.3 us -> 21.3 us
  local copies, waits for them, and re-layouts: 5.59 us -> 2.73 us
  Pallas kernels: 4.42 us -> 5.66 us
    all_to_all x1 -> x0, blocking collectives: 18 us -> none  [local(): arrived = lax.all_to_all(outgoing, ('y', 'z'), 1, 1, tiled=True)]
    ppermute x0 -> x3, starting transfers between devices: none -> 11.4 us  [local(): lax.ppermute(packed, 'pair', [((i + k) % ring, i) for i in range(ring)])]
    all_to_all x1 -> x2, starting transfers between devices: 10.9 us -> 22 us  [the longest x1 16.3 us: local(): lax.all_to_all(ask(window, peers, tile_column, block_symmetry), ('y', 'z'...]
    all_to_all x1 -> x2, waiting for transfers between devices: 10.8 us -> 20.4 us  [the longest x1 13.6 us: local(): arrived = lax.all_to_all(outgoing, ('y', 'z'), 1, 1, tiled=True)]
    ppermute x1, starting transfers between devices: 8.79 us -> 3.7 us  [local(): other = lax.ppermute(own, 'core', [(0, 1), (1, 0)])]
    all_to_all x1, blocking collectives: 35.5 us -> 30.7 us  [local(): received = lax.all_to_all(rows, ('core', 'y', 'z'), 1, 1, tiled=True)]
    all_gather x1 -> x0, waiting for transfers between devices: 4.51 us -> none  [local(): gathered = lax.all_gather(packed, 'pair', axis=0, tiled=False)]
    unnamed x6 -> x4, local copies, waits for them, and re-layouts: 4.27 us -> 1.29 us
  transfers between devices with their start and end apart: 3 -> 6, of which waited for: 2 -> 3; matrix products, arithmetic and copies ran while one was open for 1% -> 1% of each run, Pallas kernels for 0% -> 2%
where the time goes in v2:
time: 98.7 us; the launch traced here: 98.2 us
  starting transfers between devices  37.1 us (38%)
  blocking collectives  30.7 us (31%)
  waiting for transfers between devices  21.3 us (22%)
  Pallas kernels  5.66 us (6%)
  local copies, waits for them, and re-layouts  2.73 us (3%)
    all_to_all x1, blocking collectives, local(): received = lax.all_to_all(rows, ('core', 'y', 'z'), 1, 1, tiled=True)  30.7 us
    all_to_all x1, starting transfers between devices, local(): lax.all_to_all(ask(window, peers, tile_column, block_symmetry), ('y', 'z'...  16.3 us
    all_to_all x1, waiting for transfers between devices, local(): arrived = lax.all_to_all(outgoing, ('y', 'z'), 1, 1, tiled=True)  13.6 us
    ppermute x3, starting transfers between devices, local(): lax.ppermute(packed, 'pair', [((i + k) % ring, i) for i in range(ring)])  11.4 us
    all_to_all x1, waiting for transfers between devices, local(): lax.all_to_all(ask(window, peers, tile_column, block_symmetry), ('y', 'z'...  6.74 us
    all_to_all x1, starting transfers between devices, local(): arrived = lax.all_to_all(outgoing, ('y', 'z'), 1, 1, tiled=True)  5.69 us
    ppermute x1, starting transfers between devices, local(): other = lax.ppermute(own, 'core', [(0, 1), (1, 0)])  3.7 us
    pallas_call x1, Pallas kernels, contract(): pl.pallas_call(functools.partial(contract_kernel, depth, columns), out_sh...  2.16 us
  transfers between devices with their start and end apart: 6, of which 3 were waited for; matrix products, arithmetic and copies ran while one was open for 1% of the time, Pallas kernels for 2%

profile of v2, /device:TPU:1, one launch (start us, length us, event | category | flops | bytes accessed | tf_op | source)
XLA Modules:
  0.0 98.2 jit_solution(14026508156135174480)
XLA Ops:
  0.0 0.0 copy-start
  0.0 1.3 %copy-done = bf16[6,200,400]{2,1,0:T(8,128)(2,1)S(1)} copy-done((bf16[6,200,400]{2,1,0:T(8,128)(2,1)S(1)}, bf16[6,200,400]{2,1,0:T(8,128)(2,1)}, u32[]{:S(2)}) %copy-start) | copy-done | bytes 960024
  1.3 0.0 copy-start.1
  1.3 0.2 pack_integrals.1.refs_0_
  1.5 3.9 %collective-permute-start.3 = (bf16[3760,128]{1,0:T(8,128)(2,1)S(1)}, bf16[3760,128]{1,0:T(8,128)(2,1)S(1)}, u32[]{:S(2)}, u32[]{:S(2)}) collective-permute-start(bf16[3760,128]{1,0:T(8,128)(2,1)S(1)} %pack_integrals.1.refs_0_), channel_id=1, source_target_pairs={{3,0},{0,1},{1,2},{2,3},{7,4},{4,5},{5,6},{6,7},{11,8},{8,9},{9,10... | collective-permute-start | bytes 2887688 | tf_op jit(solution)/shard_map/ppermute | solution.py:236
  5.5 4.4 %collective-permute-start.2 = (bf16[3760,128]{1,0:T(8,128)(2,1)S(1)}, bf16[3760,128]{1,0:T(8,128)(2,1)S(1)}, u32[]{:S(2)}, u32[]{:S(2)}) collective-permute-start(bf16[3760,128]{1,0:T(8,128)(2,1)S(1)} %pack_integrals.1.refs_0_), channel_id=1, source_target_pairs={{2,0},{3,1},{0,2},{1,3},{6,4},{7,5},{4,6},{5,7},{10,8},{11,9},{8,1... | collective-permute-start | bytes 2887688 | tf_op jit(solution)/shard_map/ppermute | solution.py:236
  9.8 3.1 %collective-permute-start.1 = (bf16[3760,128]{1,0:T(8,128)(2,1)S(1)}, bf16[3760,128]{1,0:T(8,128)(2,1)}, u32[]{:S(2)}, u32[]{:S(2)}) collective-permute-start(bf16[3760,128]{1,0:T(8,128)(2,1)S(1)} %pack_integrals.1.refs_0_), channel_id=1, source_target_pairs={{1,0},{2,1},{3,2},{0,3},{5,4},{6,5},{7,6},{4,7},{9,8},{10,9},{11,1... | collective-permute-start | bytes 2887688 | tf_op jit(solution)/shard_map/ppermute | solution.py:236
  13.5 1.4 %ask_pieces.1 = bf16[64,8,128]{2,1,0:T(8,128)(2,1)} custom-call(s32[6]{0:T(128)} %column_ref.1, s32[1]{0:T(128)S(6)} %copy.9.symmetry_ref), custom_call_target="tpu_custom_call" | custom-call | tf_op jit(solution)/shard_map/ask_pieces/pallas_call | solution.py:80
  14.9 16.3 %all-to-all-start = ((bf16[64,8,128]{2,1,0:T(8,128)(2,1)}), bf16[64,8,128]{2,1,0:T(8,128)(2,1)S(1)}, u32[]{:S(2)}, u32[]{:S(2)}) async-start(bf16[64,8,128]{2,1,0:T(8,128)(2,1)} %ask_pieces.1), calls=%async_computation | async-start | bytes 262144 | tf_op jit(solution)/shard_map/all_to_all | solution.py:230
  31.2 0.0 copy-done.1
  31.2 3.7 %collective-permute-start = (bf16[48,800]{1,0:T(8,128)(2,1)S(1)}, bf16[48,800]{1,0:T(8,128)(2,1)S(1)}, u32[]{:S(2)}, u32[]{:S(2)}) collective-permute-start(bf16[48,800]{1,0:T(8,128)(2,1)S(1)} %bitcast.6), channel_id=1, source_target_pairs={{0,4},{4,0},{1,5},{5,1},{2,6},{6,2},{3,7},{7,3},{8,12},{12,8},{9,1... | collective-permute-start | bytes 230408 | tf_op jit(solution)/shard_map/ppermute | solution.py:233
  34.9 0.9 collective-permute-done.other_ref
  35.8 0.1 build_table.1.table_ref
  36.0 6.7 %all-to-all-done.asked_ref = bf16[64,8,128]{2,1,0:T(8,128)(2,1)S(1)} async-done(((bf16[64,8,128]{2,1,0:T(8,128)(2,1)}), bf16[64,8,128]{2,1,0:T(8,128)(2,1)S(1)}, u32[]{:S(2)}, u32[]{:S(2)}) %all-to-all-start) | async-done | bytes 131104 | tf_op jit(solution)/shard_map/all_to_all | solution.py:230
  42.7 0.7 select_pieces.1
  43.5 1.0 copy.5
  44.4 5.7 %all-to-all-start.1 = ((bf16[20,64,128]{2,0,1:T(8,128)(2,1)}), bf16[20,64,128]{2,0,1:T(8,128)(2,1)S(1)}, u32[]{:S(2)}, u32[]{:S(2)}) async-start(bf16[20,64,128]{2,0,1:T(8,128)(2,1)} %copy.5), calls=%async_computation.1 | async-start | bytes 786432 | tf_op jit(solution)/shard_map/all_to_all | solution.py:239
  50.1 13.6 %all-to-all-done.1 = bf16[20,64,128]{2,0,1:T(8,128)(2,1)S(1)} async-done(((bf16[20,64,128]{2,0,1:T(8,128)(2,1)}), bf16[20,64,128]{2,0,1:T(8,128)(2,1)S(1)}, u32[]{:S(2)}, u32[]{:S(2)}) %all-to-all-start.1) | async-done | bytes 327712 | tf_op jit(solution)/shard_map/all_to_all | solution.py:239
  63.8 0.1 copy.6.a_ref
  63.8 0.0 collective-permute-done.3.refs_3_
  63.8 0.0 collective-permute-done.2.refs_2_
  63.8 0.0 collective-permute-done.1.refs_1_
  63.9 2.2 %contract.1 = bf16[13,128,128]{2,1,0:T(8,128)(2,1)S(1)} custom-call(s32[1]{0:T(128)} %bitcast.me_ref, bf16[20,64,128]{2,1,0:T(8,128)(2,1)S(1)} %copy.6.a_ref, bf16[3760,128]{1,0:T(8,128)(2,1)S(1)} %pack_integrals.1.refs_0_, bf16[3760,128]{1,0:T(8,128)(2,1)} %collective-permute-done.1.refs_1_, bf16[3760,128]{1,0:T(8,128)(2,1)S(1)} %collective-permute-done.2.refs_2_, ...), custom_call_target="tpu_custom_call" | custom-call | tf_op jit(solution)/shard_map/contract/pallas_call | solution.py:177
  66.0 0.3 copy.7
  66.3 30.7 %all_to_all.15 = bf16[13,128,128]{2,0,1:T(8,128)(2,1)S(1)} all-to-all(bf16[13,128,128]{2,0,1:T(8,128)(2,1)S(1)} %copy.7), channel_id=1, replica_groups=mesh['y'=8,'z'=8,'core'=2,'pair'=4] {'core','y','z'}, dimensions={1} | all-to-all | bytes 851968 | tf_op jit(solution)/shard_map/all_to_all | solution.py:241
  97.0 0.1 copy.8.r_ref
  97.1 1.1 %place_rows.1 = bf16[1600,128]{1,0:T(8,128)(2,1)} custom-call(bf16[13,128,128]{2,1,0:T(8,128)(2,1)S(1)} %copy.8.r_ref), custom_call_target="tpu_custom_call" | custom-call | tf_op jit(solution)/shard_map/place_rows/pallas_call | solution.py:212
Async XLA Ops:
  0.0 1.3 %copy-start = (bf16[6,200,400]{2,1,0:T(8,128)(2,1)S(1)}, bf16[6,200,400]{2,1,0:T(8,128)(2,1)}, u32[]{:S(2)}) copy-start(bf16[6,200,400]{2,1,0:T(8,128)(2,1)} %w_ref.1) | copy-start | bytes 2880004
  1.3 29.9 %copy-start.1 = (bf16[48,1,800]{2,0,1:T(8,128)(2,1)S(1)}, bf16[48,1,800]{2,0,1:T(8,128)(2,1)}, u32[]{:S(2)}) copy-start(bf16[48,1,800]{2,0,1:T(8,128)(2,1)} %param.4) | copy-start | bytes 230404
  1.5 62.3 %collective-permute-start.3 = (bf16[3760,128]{1,0:T(8,128)(2,1)S(1)}, bf16[3760,128]{1,0:T(8,128)(2,1)S(1)}, u32[]{:S(2)}, u32[]{:S(2)}) collective-permute-start(bf16[3760,128]{1,0:T(8,128)(2,1)S(1)} %pack_integrals.1.refs_0_), channel_id=1, source_target_pairs={{3,0},{0,1},{1,2},{2,3},{7,4},{4,5},{5,6},{6,7},{11,8},{8,9},{9,10... | collective-permute-start | bytes 2887688 | tf_op jit(solution)/shard_map/ppermute | solution.py:236
  5.5 58.4 %collective-permute-start.2 = (bf16[3760,128]{1,0:T(8,128)(2,1)S(1)}, bf16[3760,128]{1,0:T(8,128)(2,1)S(1)}, u32[]{:S(2)}, u32[]{:S(2)}) collective-permute-start(bf16[3760,128]{1,0:T(8,128)(2,1)S(1)} %pack_integrals.1.refs_0_), channel_id=1, source_target_pairs={{2,0},{3,1},{0,2},{1,3},{6,4},{7,5},{4,6},{5,7},{10,8},{11,9},{8,1... | collective-permute-start | bytes 2887688 | tf_op jit(solution)/shard_map/ppermute | solution.py:236
  9.8 54.0 %collective-permute-start.1 = (bf16[3760,128]{1,0:T(8,128)(2,1)S(1)}, bf16[3760,128]{1,0:T(8,128)(2,1)}, u32[]{:S(2)}, u32[]{:S(2)}) collective-permute-start(bf16[3760,128]{1,0:T(8,128)(2,1)S(1)} %pack_integrals.1.refs_0_), channel_id=1, source_target_pairs={{1,0},{2,1},{3,2},{0,3},{5,4},{6,5},{7,6},{4,7},{9,8},{10,9},{11,1... | collective-permute-start | bytes 2887688 | tf_op jit(solution)/shard_map/ppermute | solution.py:236
  14.9 27.8 %all-to-all-start = ((bf16[64,8,128]{2,1,0:T(8,128)(2,1)}), bf16[64,8,128]{2,1,0:T(8,128)(2,1)S(1)}, u32[]{:S(2)}, u32[]{:S(2)}) async-start(bf16[64,8,128]{2,1,0:T(8,128)(2,1)} %ask_pieces.1), calls=%async_computation | async-start | bytes 262144 | tf_op jit(solution)/shard_map/all_to_all | solution.py:230
  31.2 4.6 %collective-permute-start = (bf16[48,800]{1,0:T(8,128)(2,1)S(1)}, bf16[48,800]{1,0:T(8,128)(2,1)S(1)}, u32[]{:S(2)}, u32[]{:S(2)}) collective-permute-start(bf16[48,800]{1,0:T(8,128)(2,1)S(1)} %bitcast.6), channel_id=1, source_target_pairs={{0,4},{4,0},{1,5},{5,1},{2,6},{6,2},{3,7},{7,3},{8,12},{12,8},{9,1... | collective-permute-start | bytes 230408 | tf_op jit(solution)/shard_map/ppermute | solution.py:233
  44.4 19.3 %all-to-all-start.1 = ((bf16[20,64,128]{2,0,1:T(8,128)(2,1)}), bf16[20,64,128]{2,0,1:T(8,128)(2,1)S(1)}, u32[]{:S(2)}, u32[]{:S(2)}) async-start(bf16[20,64,128]{2,0,1:T(8,128)(2,1)} %copy.5), calls=%async_computation.1 | async-start | bytes 786432 | tf_op jit(solution)/shard_map/all_to_all | solution.py:239

commit v3 on v2

--- a/solution.py
+++ b/solution.py
@@ -1,4 +1,5 @@
 import functools
+import math
 
 import jax
 import jax.numpy as jnp
@@ -15,24 +16,55 @@
 MIDDLE = 64
 LAST = 8
 
-def pack_kernel(w_ref, out_ref):
+TILE = ("y4", "y2", "y1", "z4", "z2", "z1", "core")
+SERVED = ("z1", "z2", "z4", "y1", "y2", "y4")
+
+def pack_kernel(window, w_hbm, column_hbm, symmetry_hbm, out_ref, ask_ref, w_ref, column_ref, symmetry_ref, arrivals):
     slots, width, columns = w_ref.shape
+    scalars = [
+        pltpu.make_async_copy(column_hbm, column_ref, arrivals.at[slots]),
+        pltpu.make_async_copy(symmetry_hbm, symmetry_ref, arrivals.at[slots + 1]),
+    ]
+    tiles = [pltpu.make_async_copy(w_hbm.at[k], w_ref.at[k], arrivals.at[k]) for k in range(slots)]
+    for copy in scalars + tiles:
+        copy.start()
+
+    for copy in scalars:
+        copy.wait()
+    peers, tile, _ = ask_ref.shape
+    lanes = lax.broadcasted_iota(jnp.int32, (tile, LANES), 1)
+    row = jnp.zeros((tile, LANES), F32)
+    for k in range(slots):
+        column = column_ref[k]
+        irrep = sum((column >= h * (window // 4)).astype(jnp.int32) for h in (1, 2, 3))
+        place = jnp.bitwise_xor(symmetry_ref[0], irrep) * window + column
+        row = jnp.where(lanes == k, place.astype(F32), row)
+    row = row.astype(BF16)
+    for j in range(peers):
+        ask_ref[j] = row
+
     depth = slots * width
     slabs = columns // LANES
     left = columns - slabs * LANES
-
-    def ordered(lo, hi):
-        heads = [w_ref[k, :HEAD, lo:hi] for k in range(slots)]
-        middles = [w_ref[k, HEAD : HEAD + MIDDLE, lo:hi] for k in range(slots)]
-        ends = [w_ref[k, HEAD + MIDDLE :, lo:hi].astype(F32) for k in range(slots)]
-        return heads + middles + [jnp.concatenate(ends, axis=0).astype(BF16)]
+    for k in range(slots):
+        tiles[k].wait()
+        for s in range(slabs):
+            lo, hi = s * LANES, (s + 1) * LANES
+            at = s * depth + k * HEAD
+            out_ref[at : at + HEAD, :] = w_ref[k, :HEAD, lo:hi]
+            at = s * depth + slots * HEAD + k * MIDDLE
+            out_ref[at : at + MIDDLE, :] = w_ref[k, HEAD : HEAD + MIDDLE, lo:hi]
+
+    def ends(lo, hi):
+        return jnp.concatenate([w_ref[k, HEAD + MIDDLE :, lo:hi].astype(F32) for k in range(slots)], axis=0).astype(BF16)
 
     for s in range(slabs):
-        at = s * depth
-        for part in ordered(s * LANES, (s + 1) * LANES):
-            out_ref[at : at + part.shape[0], :] = part
-            at += part.shape[0]
-    narrow = jnp.concatenate(ordered(slabs * LANES, columns), axis=0)
+        at = s * depth + slots * (HEAD + MIDDLE)
+        out_ref[at : at + slots * LAST, :] = ends(s * LANES, (s + 1) * LANES)
+    lo, hi = slabs * LANES, columns
+    narrow = [w_ref[k, :HEAD, lo:hi] for k in range(slots)]
+    narrow += [w_ref[k, HEAD : HEAD + MIDDLE, lo:hi] for k in range(slots)]
+    narrow = jnp.concatenate(narrow + [ends(lo, hi)], axis=0)
     eye = (
         lax.broadcasted_iota(jnp.int32, (left, left), 0) == lax.broadcasted_iota(jnp.int32, (left, left), 1)
     ).astype(BF16)
@@ -44,46 +76,31 @@
         out_ref[at : at + left, :] = turned[:, j * LANES : (j + 1) * LANES]
 
 
-def pack(integrals):
+def pack(window, peers, integrals, tile_column, block_symmetry):
     slots, width, columns = integrals.shape
     slabs = columns // LANES
     left = columns - slabs * LANES
     depth = slots * width
     rows = slabs * depth + -(-depth // LANES) * left
-    whole = pl.BlockSpec(memory_space=pltpu.VMEM)
-    return pl.pallas_call(
-        pack_kernel,
-        out_shape=jax.ShapeDtypeStruct((rows, LANES), BF16),
-        in_specs=[whole],
-        out_specs=whole,
-        compiler_params=pltpu.CompilerParams(vmem_limit_bytes=24 << 20),
+    anywhere = pl.BlockSpec(memory_space=pl.ANY)
+    whole = pl.BlockSpec(memory_space=pltpu.VMEM)
+    return pl.pallas_call(
+        functools.partial(pack_kernel, window),
+        out_shape=[
+            jax.ShapeDtypeStruct((rows, LANES), BF16),
+            jax.ShapeDtypeStruct((peers, 8, LANES), BF16),
+        ],
+        in_specs=[anywhere, anywhere, anywhere],
+        out_specs=[whole, whole],
+        scratch_shapes=[
+            pltpu.VMEM(integrals.shape, BF16),
+            pltpu.SMEM(tile_column.shape, jnp.int32),
+            pltpu.SMEM(block_symmetry.shape, jnp.int32),
+            pltpu.SemaphoreType.DMA((slots + 2,)),
+        ],
+        compiler_params=pltpu.CompilerParams(vmem_limit_bytes=60 << 20),
         name="pack_integrals",
-    )(integrals)
-
-
-def ask_kernel(window, column_ref, symmetry_ref, out_ref):
-    peers, tile, _ = out_ref.shape
-    lanes = lax.broadcasted_iota(jnp.int32, (tile, LANES), 1)
-    row = jnp.zeros((tile, LANES), F32)
-    for k in range(column_ref.shape[0]):
-        column = column_ref[k]
-        irrep = sum((column >= h * (window // 4)).astype(jnp.int32) for h in (1, 2, 3))
-        place = jnp.bitwise_xor(symmetry_ref[0], irrep) * window + column
-        row = jnp.where(lanes == k, place.astype(F32), row)
-    row = row.astype(BF16)
-    for j in range(peers):
-        out_ref[j] = row
-
-
-def ask(window, peers, tile_column, block_symmetry):
-    scalars = pl.BlockSpec(memory_space=pltpu.SMEM)
-    return pl.pallas_call(
-        functools.partial(ask_kernel, window),
-        out_shape=jax.ShapeDtypeStruct((peers, 8, LANES), BF16),
-        in_specs=[scalars, scalars],
-        out_specs=pl.BlockSpec(memory_space=pltpu.VMEM),
-        name="ask_pieces",
-    )(tile_column, block_symmetry)
+    )(integrals, tile_column, block_symmetry)
 
 
 def table_kernel(core_ref, own_ref, other_ref, out_ref):
@@ -158,7 +175,7 @@
     a = jnp.concatenate(halves, axis=0)
     tails[...] = jnp.zeros_like(tails)
     for step, part in enumerate(parts):
-        p = lax.rem(me_ref[0] + step, ring)
+        p = jnp.bitwise_xor(me_ref[0], (0, *(1, 2, 3))[step])
         wide = jnp.concatenate([part[s * depth : (s + 1) * depth, :] for s in range(slabs)], axis=1)
         product = jnp.dot(a[:, :depth], wide, preferred_element_type=F32).astype(BF16)
         for s in range(slabs):
@@ -185,14 +202,16 @@
     )(me, arrived, *parts)
 
 
-def place_kernel(columns, r_ref, out_ref):
+def place_kernel(columns, sizes, r_ref, out_ref):
     count, blocks, _ = r_ref.shape
-    half = blocks // 2
     slabs = columns // LANES
     left = columns - slabs * LANES
     came = lax.broadcasted_iota(jnp.int32, (blocks, blocks), 0)
     goes = lax.broadcasted_iota(jnp.int32, (blocks, blocks), 1)
-    order = jnp.where(came < half, 2 * came, 2 * (came - half) + 1)
+    order, rest = jnp.zeros_like(came), came
+    for axis in reversed(("core", *SERVED)):
+        order += rest % sizes[axis] * math.prod(sizes[a] for a in TILE[TILE.index(axis) + 1 :])
+        rest = rest // sizes[axis]
     turn = (order == goes).astype(F32).astype(BF16)
     for j in range(count):
         block = lax.dot_general(r_ref[j], turn, (((0,), (0,)), ((), ())), preferred_element_type=F32).astype(BF16)
@@ -205,12 +224,12 @@
                 out_ref[at : at + left, :] = block[p * left : (p + 1) * left]
 
 
-def place(columns, received):
+def place(columns, sizes, received):
     count, blocks, _ = received.shape
     ring = (count - 1) // (columns // LANES)
     whole = pl.BlockSpec(memory_space=pltpu.VMEM)
     return pl.pallas_call(
-        functools.partial(place_kernel, columns),
+        functools.partial(place_kernel, columns, sizes),
         out_shape=jax.ShapeDtypeStruct((ring * columns, blocks), BF16),
         in_specs=[whole],
         out_specs=whole,
@@ -224,28 +243,27 @@
     slots, width, columns = integrals.shape
     depth = slots * width
     ring = lax.axis_size("pair")
-    peers = lax.axis_size("y") * lax.axis_size("z")
-
-    packed = pack(integrals)
-    asked = lax.all_to_all(ask(window, peers, tile_column, block_symmetry), ("y", "z"), 0, 0, tiled=True)
-
+    sizes = {axis: lax.axis_size(axis) for axis in TILE}
+    peers = math.prod(sizes[axis] for axis in SERVED)
+
+    packed, wanted = pack(window, peers, integrals, tile_column, block_symmetry)
+    asked = lax.all_to_all(wanted, SERVED, 0, 0, tiled=True)
     own = amplitudes.reshape(window, virtuals)
     other = lax.ppermute(own, "core", [(0, 1), (1, 0)])
     table = build_table(lax.axis_index("core").reshape(1), own, other)
     parts = [packed]
-    parts += [lax.ppermute(packed, "pair", [((i + k) % ring, i) for i in range(ring)]) for k in range(1, ring)]
+    parts += [lax.ppermute(packed, "pair", [(i ^ k, i) for i in range(ring)]) for k in (1, 2, 3)]
 
     outgoing = select(slots, table, asked)
-    arrived = lax.all_to_all(outgoing, ("y", "z"), 1, 1, tiled=True)
+    arrived = lax.all_to_all(outgoing, SERVED, 1, 1, tiled=True)
     rows = contract(depth, columns, lax.axis_index("pair").reshape(1), arrived, parts)
-    received = lax.all_to_all(rows, ("core", "y", "z"), 1, 1, tiled=True)
-    return place(columns, received).T[None]
+    received = lax.all_to_all(rows, ("core", *SERVED), 1, 1, tiled=True)
+    return place(columns, sizes, received).T[None]
 
 
 def solution(mesh):
-    sizes = {2: (1, 1), 8: (2, 2), 128: (8, 8)}[mesh.shape["tile"]]
-    fine = Mesh(mesh.devices.reshape(*sizes, 2, mesh.shape["pair"]), ("y", "z", "core", "pair"))
-    tile = ("y", "z", "core")
-    in_specs = (P(None, (*tile, "pair"), None), P(tile, None, "pair"), P(tile), P(tile))
-    out_specs = P((*tile, "pair"), None, None)
+    cut = {8: (1, 1, 2, 1, 1, 2, 2), 16: (1, 2, 2, 1, 1, 2, 2), 128: (2,) * 7}[mesh.shape["tile"]]
+    fine = Mesh(mesh.devices.reshape(*cut, mesh.shape["pair"]), (*TILE, "pair"))
+    in_specs = (P(None, (*TILE, "pair"), None), P(TILE, None, "pair"), P(TILE), P(TILE))
+    out_specs = P((*TILE, "pair"), None, None)
     return jax.shard_map(local, mesh=fine, in_specs=in_specs, out_specs=out_specs, check_vma=False)

time: 98.7 us -> 95.1 us (0.964)
  blocking collectives: 30.7 us -> 27.7 us
  starting transfers between devices: 37.1 us -> 35.3 us
  waiting for transfers between devices: 21.3 us -> 22.6 us
  local copies, waits for them, and re-layouts: 2.73 us -> 1.44 us
  Pallas kernels: 5.66 us -> 6.85 us
    all_to_all x1, blocking collectives: 30.7 us -> 27.7 us  [local(): received = lax.all_to_all(rows, ('core', *SERVED), 1, 1, tiled=True)]
    ppermute x3, starting transfers between devices: 11.4 us -> 9.62 us  [local(): lax.ppermute(packed, 'pair', [(i ^ k, i) for i in range(ring)])]
    unnamed x4, local copies, waits for them, and re-layouts: 1.29 us -> 0.01 us
    all_to_all x2, waiting for transfers between devices: 20.4 us -> 21.6 us  [the longest x1 14.8 us: local(): arrived = lax.all_to_all(outgoing, SERVED, 1, 1, tiled=True)]
    pallas_call x3 -> x2, Pallas kernels: 2.63 us -> 3.83 us  [the longest x1 2.6 us: pack(): pl.pallas_call(functools.partial(pack_kernel, window), out_shape=[jax.Sha...]
  transfers between devices with their start and end apart: 6 -> 6, of which waited for: 3 -> 3; matrix products, arithmetic and copies ran while one was open for 1% -> 1% of each run, Pallas kernels for 2% -> 1%
where the time goes in v3:
time: 95.1 us; the launch traced here: 94.6 us
  starting transfers between devices  35.3 us (37%)
  blocking collectives  27.7 us (29%)
  waiting for transfers between devices  22.6 us (24%)
  Pallas kernels  6.85 us (7%)
  local copies, waits for them, and re-layouts  1.44 us (2%)
    all_to_all x1, blocking collectives, local(): received = lax.all_to_all(rows, ('core', *SERVED), 1, 1, tiled=True)  27.7 us
    all_to_all x1, starting transfers between devices, local(): asked = lax.all_to_all(wanted, SERVED, 0, 0, tiled=True)  16.5 us
    all_to_all x1, waiting for transfers between devices, local(): arrived = lax.all_to_all(outgoing, SERVED, 1, 1, tiled=True)  14.8 us
    ppermute x3, starting transfers between devices, local(): lax.ppermute(packed, 'pair', [(i ^ k, i) for i in range(ring)])  9.62 us
    all_to_all x1, waiting for transfers between devices, local(): asked = lax.all_to_all(wanted, SERVED, 0, 0, tiled=True)  6.87 us
    all_to_all x1, starting transfers between devices, local(): arrived = lax.all_to_all(outgoing, SERVED, 1, 1, tiled=True)  5.43 us
    ppermute x1, starting transfers between devices, local(): other = lax.ppermute(own, 'core', [(0, 1), (1, 0)])  3.7 us
    pallas_call x1, Pallas kernels, pack(): pl.pallas_call(functools.partial(pack_kernel, window), out_shape=[jax.Sha...  2.6 us
  transfers between devices with their start and end apart: 6, of which 3 were waited for; matrix products, arithmetic and copies ran while one was open for 1% of the time, Pallas kernels for 1%

profile of v3, /device:TPU:1, one launch (start us, length us, event | category | flops | bytes accessed | tf_op | source)
XLA Modules:
  0.0 94.6 jit_solution(12554323710347004683)
XLA Ops:
  0.0 0.0 copy-start.1
  0.7 2.6 %pack_integrals.1 = (bf16[3760,128]{1,0:T(8,128)(2,1)}, bf16[64,8,128]{2,1,0:T(8,128)(2,1)}) custom-call(bf16[6,200,400]{2,1,0:T(8,128)(2,1)} %w_hbm.1, s32[6]{0:T(128)} %column_hbm.1, s32[1]{0:T(128)S(6)} %copy.9.symmetry_hbm), custom_call_target="tpu_custom_call" | custom-call | tf_op jit(solution)/shard_map/pack_integrals/pallas_call | solution.py:87
  3.3 5.2 %collective-permute-start.3 = (bf16[3760,128]{1,0:T(8,128)(2,1)}, bf16[3760,128]{1,0:T(8,128)(2,1)S(1)}, u32[]{:S(2)}, u32[]{:S(2)}) collective-permute-start(bf16[3760,128]{1,0:T(8,128)(2,1)} %get-tuple-element.8.refs_0_), channel_id=1, source_target_pairs={{3,0},{2,1},{1,2},{0,3},{7,4},{6,5},{5,6},{4,7},{11,8},{10,9},{9,1... | collective-permute-start | bytes 2887688 | tf_op jit(solution)/shard_map/ppermute | solution.py:255
  8.5 2.4 %collective-permute-start.2 = (bf16[3760,128]{1,0:T(8,128)(2,1)}, bf16[3760,128]{1,0:T(8,128)(2,1)S(1)}, u32[]{:S(2)}, u32[]{:S(2)}) collective-permute-start(bf16[3760,128]{1,0:T(8,128)(2,1)} %get-tuple-element.8.refs_0_), channel_id=1, source_target_pairs={{2,0},{3,1},{0,2},{1,3},{6,4},{7,5},{4,6},{5,7},{10,8},{11,9},{8,1... | collective-permute-start | bytes 2887688 | tf_op jit(solution)/shard_map/ppermute | solution.py:255
  11.0 2.0 %collective-permute-start.1 = (bf16[3760,128]{1,0:T(8,128)(2,1)}, bf16[3760,128]{1,0:T(8,128)(2,1)}, u32[]{:S(2)}, u32[]{:S(2)}) collective-permute-start(bf16[3760,128]{1,0:T(8,128)(2,1)} %get-tuple-element.8.refs_0_), channel_id=1, source_target_pairs={{1,0},{0,1},{3,2},{2,3},{5,4},{4,5},{7,6},{6,7},{9,8},{8,9},{11,10... | collective-permute-start | bytes 2887688 | tf_op jit(solution)/shard_map/ppermute | solution.py:255
  12.9 16.5 %all-to-all-start = ((bf16[64,8,128]{2,1,0:T(8,128)(2,1)}), bf16[64,8,128]{2,1,0:T(8,128)(2,1)S(1)}, u32[]{:S(2)}, u32[]{:S(2)}) async-start(bf16[64,8,128]{2,1,0:T(8,128)(2,1)} %get-tuple-element.7), calls=%async_computation | async-start | bytes 262144 | tf_op jit(solution)/shard_map/all_to_all | solution.py:250
  29.5 0.0 copy-done.1
  29.5 3.7 %collective-permute-start = (bf16[48,800]{1,0:T(8,128)(2,1)S(1)}, bf16[48,800]{1,0:T(8,128)(2,1)S(1)}, u32[]{:S(2)}, u32[]{:S(2)}) collective-permute-start(bf16[48,800]{1,0:T(8,128)(2,1)S(1)} %bitcast.6), channel_id=1, source_target_pairs={{0,4},{4,0},{1,5},{5,1},{2,6},{6,2},{3,7},{7,3},{8,12},{12,8},{9,1... | collective-permute-start | bytes 230408 | tf_op jit(solution)/shard_map/ppermute | solution.py:252
  33.2 0.9 collective-permute-done.other_ref
  34.1 0.1 build_table.1.table_ref
  34.2 6.9 %all-to-all-done.asked_ref = bf16[64,8,128]{2,1,0:T(8,128)(2,1)S(1)} async-done(((bf16[64,8,128]{2,1,0:T(8,128)(2,1)}), bf16[64,8,128]{2,1,0:T(8,128)(2,1)S(1)}, u32[]{:S(2)}, u32[]{:S(2)}) %all-to-all-start) | async-done | bytes 131104 | tf_op jit(solution)/shard_map/all_to_all | solution.py:250
  41.1 0.7 select_pieces.1
  41.8 0.0 copy-start
  41.8 1.0 %copy.5 = bf16[20,64,128]{2,0,1:T(8,128)(2,1)} copy(bf16[20,64,128]{2,1,0:T(8,128)(2,1)S(1)} %select_pieces.1) | data formatting | bytes 655360 | tf_op jit(solution)/shard_map/select_pieces/pallas_call | solution.py:158
  42.8 5.4 %all-to-all-start.1 = ((bf16[20,64,128]{2,0,1:T(8,128)(2,1)}), bf16[20,64,128]{2,0,1:T(8,128)(2,1)S(1)}, u32[]{:S(2)}, u32[]{:S(2)}) async-start(bf16[20,64,128]{2,0,1:T(8,128)(2,1)} %copy.5), calls=%async_computation.1 | async-start | bytes 786432 | tf_op jit(solution)/shard_map/all_to_all | solution.py:258
  48.2 14.8 %all-to-all-done.1 = bf16[20,64,128]{2,0,1:T(8,128)(2,1)S(1)} async-done(((bf16[20,64,128]{2,0,1:T(8,128)(2,1)}), bf16[20,64,128]{2,0,1:T(8,128)(2,1)S(1)}, u32[]{:S(2)}, u32[]{:S(2)}) %all-to-all-start.1) | async-done | bytes 327712 | tf_op jit(solution)/shard_map/all_to_all | solution.py:258
  63.0 0.1 copy.6.a_ref
  63.1 0.0 collective-permute-done.3.refs_3_
  63.1 0.0 collective-permute-done.2.refs_2_
  63.1 0.0 collective-permute-done.1.refs_1_
  63.1 0.0 copy-done
  63.1 2.2 %contract.1 = bf16[13,128,128]{2,1,0:T(8,128)(2,1)S(1)} custom-call(s32[1]{0:T(128)} %bitcast.me_ref, bf16[20,64,128]{2,1,0:T(8,128)(2,1)S(1)} %copy.6.a_ref, bf16[3760,128]{1,0:T(8,128)(2,1)S(1)} %copy-done, bf16[3760,128]{1,0:T(8,128)(2,1)} %collective-permute-done.1.refs_1_, bf16[3760,128]{1,0:T(8,128)(2,1)S(1)} %collective-permute-done.2.refs_2_, ...), custom_call_target="tpu_custom_call" | custom-call | tf_op jit(solution)/shard_map/contract/pallas_call | solution.py:194
  65.3 0.3 copy.7
  65.6 27.7 %all_to_all.15 = bf16[13,128,128]{2,0,1:T(8,128)(2,1)S(1)} all-to-all(bf16[13,128,128]{2,0,1:T(8,128)(2,1)S(1)} %copy.7), channel_id=1, replica_groups=mesh['y4'=2,'y2'=2,'y1'=2,'z4'=2,'z2'=2,'z1'=2,'core'=2,'pair'=4] {'core..., dimensions={1} | all-to-all | bytes 851968 | tf_op jit(solution)/shard_map/all_to_all | solution.py:260
  93.3 0.1 copy.8.r_ref
  93.4 1.2 %place_rows.1 = bf16[1600,128]{1,0:T(8,128)(2,1)} custom-call(bf16[13,128,128]{2,1,0:T(8,128)(2,1)S(1)} %copy.8.r_ref), custom_call_target="tpu_custom_call" | custom-call | tf_op jit(solution)/shard_map/place_rows/pallas_call | solution.py:231
Async XLA Ops:
  0.0 29.5 %copy-start.1 = (bf16[48,1,800]{2,0,1:T(8,128)(2,1)S(1)}, bf16[48,1,800]{2,0,1:T(8,128)(2,1)}, u32[]{:S(2)}) copy-start(bf16[48,1,800]{2,0,1:T(8,128)(2,1)} %param.4) | copy-start | bytes 230404
  3.3 59.8 %collective-permute-start.3 = (bf16[3760,128]{1,0:T(8,128)(2,1)}, bf16[3760,128]{1,0:T(8,128)(2,1)S(1)}, u32[]{:S(2)}, u32[]{:S(2)}) collective-permute-start(bf16[3760,128]{1,0:T(8,128)(2,1)} %get-tuple-element.8.refs_0_), channel_id=1, source_target_pairs={{3,0},{2,1},{1,2},{0,3},{7,4},{6,5},{5,6},{4,7},{11,8},{10,9},{9,1... | collective-permute-start | bytes 2887688 | tf_op jit(solution)/shard_map/ppermute | solution.py:255
  8.5 54.6 %collective-permute-start.2 = (bf16[3760,128]{1,0:T(8,128)(2,1)}, bf16[3760,128]{1,0:T(8,128)(2,1)S(1)}, u32[]{:S(2)}, u32[]{:S(2)}) collective-permute-start(bf16[3760,128]{1,0:T(8,128)(2,1)} %get-tuple-element.8.refs_0_), channel_id=1, source_target_pairs={{2,0},{3,1},{0,2},{1,3},{6,4},{7,5},{4,6},{5,7},{10,8},{11,9},{8,1... | collective-permute-start | bytes 2887688 | tf_op jit(solution)/shard_map/ppermute | solution.py:255
  11.0 52.2 %collective-permute-start.1 = (bf16[3760,128]{1,0:T(8,128)(2,1)}, bf16[3760,128]{1,0:T(8,128)(2,1)}, u32[]{:S(2)}, u32[]{:S(2)}) collective-permute-start(bf16[3760,128]{1,0:T(8,128)(2,1)} %get-tuple-element.8.refs_0_), channel_id=1, source_target_pairs={{1,0},{0,1},{3,2},{2,3},{5,4},{4,5},{7,6},{6,7},{9,8},{8,9},{11,10... | collective-permute-start | bytes 2887688 | tf_op jit(solution)/shard_map/ppermute | solution.py:255
  12.9 28.1 %all-to-all-start = ((bf16[64,8,128]{2,1,0:T(8,128)(2,1)}), bf16[64,8,128]{2,1,0:T(8,128)(2,1)S(1)}, u32[]{:S(2)}, u32[]{:S(2)}) async-start(bf16[64,8,128]{2,1,0:T(8,128)(2,1)} %get-tuple-element.7), calls=%async_computation | async-start | bytes 262144 | tf_op jit(solution)/shard_map/all_to_all | solution.py:250
  29.5 4.6 %collective-permute-start = (bf16[48,800]{1,0:T(8,128)(2,1)S(1)}, bf16[48,800]{1,0:T(8,128)(2,1)S(1)}, u32[]{:S(2)}, u32[]{:S(2)}) collective-permute-start(bf16[48,800]{1,0:T(8,128)(2,1)S(1)} %bitcast.6), channel_id=1, source_target_pairs={{0,4},{4,0},{1,5},{5,1},{2,6},{6,2},{3,7},{7,3},{8,12},{12,8},{9,1... | collective-permute-start | bytes 230408 | tf_op jit(solution)/shard_map/ppermute | solution.py:252
  41.8 21.3 %copy-start = (bf16[3760,128]{1,0:T(8,128)(2,1)S(1)}, bf16[3760,128]{1,0:T(8,128)(2,1)}, u32[]{:S(2)}) copy-start(bf16[3760,128]{1,0:T(8,128)(2,1)} %get-tuple-element.8.refs_0_) | copy-start | bytes 2887684
  42.8 20.2 %all-to-all-start.1 = ((bf16[20,64,128]{2,0,1:T(8,128)(2,1)}), bf16[20,64,128]{2,0,1:T(8,128)(2,1)S(1)}, u32[]{:S(2)}, u32[]{:S(2)}) async-start(bf16[20,64,128]{2,0,1:T(8,128)(2,1)} %copy.5), calls=%async_computation.1 | async-start | bytes 786432 | tf_op jit(solution)/shard_map/all_to_all | solution.py:258

commit v4 on v3

--- a/solution.py
+++ b/solution.py
@@ -17,9 +17,12 @@
 LAST = 8
 
 TILE = ("y4", "y2", "y1", "z4", "z2", "z1", "core")
-SERVED = ("z1", "z2", "z4", "y1", "y2", "y4")
-
-def pack_kernel(window, w_hbm, column_hbm, symmetry_hbm, out_ref, ask_ref, w_ref, column_ref, symmetry_ref, arrivals):
+SERVED = ("y1", "y2", "y4", "z1", "z2", "z4")
+
+PLACES = (0, 1, 2, 3)
+
+
+def pack_kernel(window, w_hbm, column_hbm, symmetry_hbm, out_hbm, ask_hbm, w_ref, column_ref, symmetry_ref, out_ref, ask_ref, arrivals, departures):
     slots, width, columns = w_ref.shape
     scalars = [
         pltpu.make_async_copy(column_hbm, column_ref, arrivals.at[slots]),
@@ -42,6 +45,8 @@
     row = row.astype(BF16)
     for j in range(peers):
         ask_ref[j] = row
+    leaving = [pltpu.make_async_copy(ask_ref, ask_hbm, departures.at[0])]
+    leaving[0].start()
 
     depth = slots * width
     slabs = columns // LANES
@@ -61,6 +66,9 @@
     for s in range(slabs):
         at = s * depth + slots * (HEAD + MIDDLE)
         out_ref[at : at + slots * LAST, :] = ends(s * LANES, (s + 1) * LANES)
+        rows = pl.ds(s * depth, depth)
+        leaving.append(pltpu.make_async_copy(out_ref.at[rows], out_hbm.at[rows], departures.at[1 + s]))
+        leaving[-1].start()
     lo, hi = slabs * LANES, columns
     narrow = [w_ref[k, :HEAD, lo:hi] for k in range(slots)]
     narrow += [w_ref[k, HEAD : HEAD + MIDDLE, lo:hi] for k in range(slots)]
@@ -74,6 +82,11 @@
     for j in range(chunks):
         at = slabs * depth + j * left
         out_ref[at : at + left, :] = turned[:, j * LANES : (j + 1) * LANES]
+    rows = pl.ds(slabs * depth, chunks * left)
+    leaving.append(pltpu.make_async_copy(out_ref.at[rows], out_hbm.at[rows], departures.at[1 + slabs]))
+    leaving[-1].start()
+    for copy in leaving:
+        copy.wait()
 
 
 def pack(window, peers, integrals, tile_column, block_symmetry):
@@ -83,7 +96,6 @@
     depth = slots * width
     rows = slabs * depth + -(-depth // LANES) * left
     anywhere = pl.BlockSpec(memory_space=pl.ANY)
-    whole = pl.BlockSpec(memory_space=pltpu.VMEM)
     return pl.pallas_call(
         functools.partial(pack_kernel, window),
         out_shape=[
@@ -91,12 +103,15 @@
             jax.ShapeDtypeStruct((peers, 8, LANES), BF16),
         ],
         in_specs=[anywhere, anywhere, anywhere],
-        out_specs=[whole, whole],
+        out_specs=[anywhere, anywhere],
         scratch_shapes=[
             pltpu.VMEM(integrals.shape, BF16),
             pltpu.SMEM(tile_column.shape, jnp.int32),
             pltpu.SMEM(block_symmetry.shape, jnp.int32),
+            pltpu.VMEM((rows, LANES), BF16),
+            pltpu.VMEM((peers, 8, LANES), BF16),
             pltpu.SemaphoreType.DMA((slots + 2,)),
+            pltpu.SemaphoreType.DMA((slabs + 2,)),
         ],
         compiler_params=pltpu.CompilerParams(vmem_limit_bytes=60 << 20),
         name="pack_integrals",
@@ -127,7 +142,7 @@
     )(core, own, other)
 
 
-def select_kernel(slots, table_ref, asked_ref, out_ref):
+def select_kernel(slots, table_ref, asked_ref, out_hbm, rows, narrow, departures):
     peers = asked_ref.shape[0]
     table = table_ref[...]
     wanted = asked_ref[...].astype(F32)[:, 0, :].astype(jnp.int32)
@@ -136,19 +151,28 @@
     for k in range(slots):
         chosen = (places == wanted[:, k : k + 1]).astype(F32).astype(BF16)
         pieces.append(jnp.dot(chosen, table, preferred_element_type=F32))
-    chunks = out_ref.shape[0] // 2
+    chunks = slots + slots // 2 + 1
     for r in range(2):
         base = r * 2 * LANES
         for k in range(slots):
-            out_ref[r * chunks + k] = pieces[k][:, base : base + LANES].astype(BF16)
+            rows[:, r * chunks + k, :] = pieces[k][:, base : base + LANES]
         for j in range(slots // 2):
             lo, hi = base + HEAD, base + HEAD + MIDDLE
             pair = [pieces[2 * j][:, lo:hi], pieces[2 * j + 1][:, lo:hi]]
-            out_ref[r * chunks + slots + j] = jnp.concatenate(pair, axis=1).astype(BF16)
+            rows[:, r * chunks + slots + j, :] = jnp.concatenate(pair, axis=1)
         lo = base + HEAD + MIDDLE
         ends = [pieces[k][:, lo : lo + LAST] for k in range(slots)]
         ends.append(jnp.zeros((peers, LANES - slots * LAST), F32))
-        out_ref[r * chunks + chunks - 1] = jnp.concatenate(ends, axis=1).astype(BF16)
+        rows[:, r * chunks + chunks - 1, :] = jnp.concatenate(ends, axis=1)
+    count = departures.shape[0]
+    leaving = []
+    for k in range(count):
+        group = pl.ds(k * (peers // count), peers // count)
+        narrow[group] = rows[group].astype(BF16)
+        leaving.append(pltpu.make_async_copy(narrow.at[group], out_hbm.at[group], departures.at[k]))
+        leaving[-1].start()
+    for copy in leaving:
+        copy.wait()
 
 
 def select(slots, table, asked):
@@ -157,9 +181,14 @@
     whole = pl.BlockSpec(memory_space=pltpu.VMEM)
     return pl.pallas_call(
         functools.partial(select_kernel, slots),
-        out_shape=jax.ShapeDtypeStruct((2 * chunks, peers, LANES), BF16),
+        out_shape=jax.ShapeDtypeStruct((peers, 2 * chunks, LANES), BF16),
         in_specs=[whole, whole],
-        out_specs=whole,
+        out_specs=pl.BlockSpec(memory_space=pl.ANY),
+        scratch_shapes=[
+            pltpu.VMEM((peers, 2 * chunks, LANES), F32),
+            pltpu.VMEM((peers, 2 * chunks, LANES), BF16),
+            pltpu.SemaphoreType.DMA((4,)),
+        ],
         compiler_params=pltpu.CompilerParams(vmem_limit_bytes=24 << 20),
         name="select_pieces",
     )(table, asked)
@@ -175,7 +204,7 @@
     a = jnp.concatenate(halves, axis=0)
     tails[...] = jnp.zeros_like(tails)
     for step, part in enumerate(parts):
-        p = jnp.bitwise_xor(me_ref[0], (0, *(1, 2, 3))[step])
+        p = jnp.bitwise_xor(me_ref[0], PLACES[step])
         wide = jnp.concatenate([part[s * depth : (s + 1) * depth, :] for s in range(slabs)], axis=1)
         product = jnp.dot(a[:, :depth], wide, preferred_element_type=F32).astype(BF16)
         for s in range(slabs):
@@ -252,10 +281,10 @@
     other = lax.ppermute(own, "core", [(0, 1), (1, 0)])
     table = build_table(lax.axis_index("core").reshape(1), own, other)
     parts = [packed]
-    parts += [lax.ppermute(packed, "pair", [(i ^ k, i) for i in range(ring)]) for k in (1, 2, 3)]
+    parts += [lax.ppermute(packed, "pair", [(i ^ k, i) for i in range(ring)]) for k in PLACES[1:]]
 
     outgoing = select(slots, table, asked)
-    arrived = lax.all_to_all(outgoing, SERVED, 1, 1, tiled=True)
+    arrived = jnp.transpose(lax.all_to_all(outgoing, SERVED, 0, 0, tiled=True), (1, 0, 2))
     rows = contract(depth, columns, lax.axis_index("pair").reshape(1), arrived, parts)
     received = lax.all_to_all(rows, ("core", *SERVED), 1, 1, tiled=True)
     return place(columns, sizes, received).T[None]

time: 95.1 us -> 94.3 us (level)
  waiting for transfers between devices: 22.6 us -> 21.3 us
  local copies, waits for them, and re-layouts: 1.44 us -> 0.47 us
    all_to_all x1, waiting for transfers between devices: 14.8 us -> 13.7 us  [local(): lax.all_to_all(outgoing, SERVED, 0, 0, tiled=True)]
    pallas_call x1 -> x0, local copies, waits for them, and re-layouts: 0.97 us -> none  [select(): pl.pallas_call(functools.partial(select_kernel, slots), out_shape=jax.Sha...]
  transfers between devices with their start and end apart: 6 -> 6, of which waited for: 3 -> 3; matrix products, arithmetic and copies ran while one was open for 1% -> 0% of each run, Pallas kernels for 1% -> 2%
where the time goes in v4:
time: 94.3 us; the launch traced here: 93.9 us
  starting transfers between devices  35.5 us (38%)
  blocking collectives  28.1 us (30%)
  waiting for transfers between devices  21.3 us (23%)
  Pallas kernels  7.65 us (8%)
    all_to_all x1, blocking collectives, local(): received = lax.all_to_all(rows, ('core', *SERVED), 1, 1, tiled=True)  28.1 us
    all_to_all x1, starting transfers between devices, local(): asked = lax.all_to_all(wanted, SERVED, 0, 0, tiled=True)  16.5 us
    all_to_all x1, waiting for transfers between devices, local(): lax.all_to_all(outgoing, SERVED, 0, 0, tiled=True)  13.7 us
    ppermute x3, starting transfers between devices, local(): lax.ppermute(packed, 'pair', [(i ^ k, i) for i in range(ring)])  9.62 us
    all_to_all x1, waiting for transfers between devices, local(): asked = lax.all_to_all(wanted, SERVED, 0, 0, tiled=True)  6.68 us
    all_to_all x1, starting transfers between devices, local(): lax.all_to_all(outgoing, SERVED, 0, 0, tiled=True)  5.64 us
    ppermute x1, starting transfers between devices, local(): other = lax.ppermute(own, 'core', [(0, 1), (1, 0)])  3.7 us
    pallas_call x1, Pallas kernels, pack(): pl.pallas_call(functools.partial(pack_kernel, window), out_shape=[jax.Sha...  2.48 us
  transfers between devices with their start and end apart: 6, of which 3 were waited for; matrix products, arithmetic and copies ran while one was open for 0% of the time, Pallas kernels for 2%

profile of v4, /device:TPU:1, one launch (start us, length us, event | category | flops | bytes accessed | tf_op | source)
XLA Modules:
  0.0 93.9 jit_solution(9547138047336386626)
XLA Ops:
  0.0 0.0 copy-start.1
  0.7 2.5 %pack_integrals.1 = (bf16[3760,128]{1,0:T(8,128)(2,1)}, bf16[64,8,128]{2,1,0:T(8,128)(2,1)}) custom-call(bf16[6,200,400]{2,1,0:T(8,128)(2,1)} %w_hbm.1, s32[6]{0:T(128)} %column_hbm.1, s32[1]{0:T(128)S(6)} %copy.11.symmetry_hbm), custom_call_target="tpu_custom_call" | custom-call | tf_op jit(solution)/shard_map/pack_integrals/pallas_call | solution.py:99
  3.2 5.2 %collective-permute-start.3 = (bf16[3760,128]{1,0:T(8,128)(2,1)}, bf16[3760,128]{1,0:T(8,128)(2,1)S(1)}, u32[]{:S(2)}, u32[]{:S(2)}) collective-permute-start(bf16[3760,128]{1,0:T(8,128)(2,1)} %get-tuple-element.8.refs_0_), channel_id=1, source_target_pairs={{3,0},{2,1},{1,2},{0,3},{7,4},{6,5},{5,6},{4,7},{11,8},{10,9},{9,1... | collective-permute-start | bytes 2887688 | tf_op jit(solution)/shard_map/ppermute | solution.py:284
  8.4 2.4 %collective-permute-start.2 = (bf16[3760,128]{1,0:T(8,128)(2,1)}, bf16[3760,128]{1,0:T(8,128)(2,1)S(1)}, u32[]{:S(2)}, u32[]{:S(2)}) collective-permute-start(bf16[3760,128]{1,0:T(8,128)(2,1)} %get-tuple-element.8.refs_0_), channel_id=1, source_target_pairs={{2,0},{3,1},{0,2},{1,3},{6,4},{7,5},{4,6},{5,7},{10,8},{11,9},{8,1... | collective-permute-start | bytes 2887688 | tf_op jit(solution)/shard_map/ppermute | solution.py:284
  10.8 2.0 %collective-permute-start.1 = (bf16[3760,128]{1,0:T(8,128)(2,1)}, bf16[3760,128]{1,0:T(8,128)(2,1)}, u32[]{:S(2)}, u32[]{:S(2)}) collective-permute-start(bf16[3760,128]{1,0:T(8,128)(2,1)} %get-tuple-element.8.refs_0_), channel_id=1, source_target_pairs={{1,0},{0,1},{3,2},{2,3},{5,4},{4,5},{7,6},{6,7},{9,8},{8,9},{11,10... | collective-permute-start | bytes 2887688 | tf_op jit(solution)/shard_map/ppermute | solution.py:284
  12.8 16.5 %all-to-all-start = ((bf16[64,8,128]{2,1,0:T(8,128)(2,1)}), bf16[64,8,128]{2,1,0:T(8,128)(2,1)S(1)}, u32[]{:S(2)}, u32[]{:S(2)}) async-start(bf16[64,8,128]{2,1,0:T(8,128)(2,1)} %get-tuple-element.7), calls=%async_computation | async-start | bytes 262144 | tf_op jit(solution)/shard_map/all_to_all | solution.py:279
  29.3 0.0 copy-done.1
  29.3 3.7 %collective-permute-start = (bf16[48,800]{1,0:T(8,128)(2,1)S(1)}, bf16[48,800]{1,0:T(8,128)(2,1)S(1)}, u32[]{:S(2)}, u32[]{:S(2)}) collective-permute-start(bf16[48,800]{1,0:T(8,128)(2,1)S(1)} %bitcast.10), channel_id=1, source_target_pairs={{0,4},{4,0},{1,5},{5,1},{2,6},{6,2},{3,7},{7,3},{8,12},{12,8},{9,1... | collective-permute-start | bytes 230408 | tf_op jit(solution)/shard_map/ppermute | solution.py:281
  33.1 0.9 collective-permute-done.other_ref
  34.0 0.0 copy-start
  34.0 0.1 build_table.1.table_ref
  34.1 6.7 %all-to-all-done.asked_ref = bf16[64,8,128]{2,1,0:T(8,128)(2,1)S(1)} async-done(((bf16[64,8,128]{2,1,0:T(8,128)(2,1)}), bf16[64,8,128]{2,1,0:T(8,128)(2,1)S(1)}, u32[]{:S(2)}, u32[]{:S(2)}) %all-to-all-start) | async-done | bytes 131104 | tf_op jit(solution)/shard_map/all_to_all | solution.py:279
  40.8 1.7 %select_pieces.1 = bf16[64,20,128]{2,1,0:T(8,128)(2,1)} custom-call(bf16[192,512]{1,0:T(8,128)(2,1)S(1)} %build_table.1.table_ref, bf16[64,8,128]{2,1,0:T(8,128)(2,1)S(1)} %all-to-all-done.asked_ref), custom_call_target="tpu_custom_call" | custom-call | tf_op jit(solution)/shard_map/select_pieces/pallas_call | solution.py:182
  42.4 5.6 %all-to-all-start.1 = ((bf16[64,20,128]{2,1,0:T(8,128)(2,1)}), bf16[64,20,128]{2,1,0:T(8,128)(2,1)S(1)}, u32[]{:S(2)}, u32[]{:S(2)}) async-start(bf16[64,20,128]{2,1,0:T(8,128)(2,1)} %select_pieces.1), calls=%async_computation.1 | async-start | bytes 786432 | tf_op jit(solution)/shard_map/all_to_all | solution.py:287
  48.1 13.7 %all-to-all-done.1 = bf16[64,20,128]{2,1,0:T(8,128)(2,1)S(1)} async-done(((bf16[64,20,128]{2,1,0:T(8,128)(2,1)}), bf16[64,20,128]{2,1,0:T(8,128)(2,1)S(1)}, u32[]{:S(2)}, u32[]{:S(2)}) %all-to-all-start.1) | async-done | bytes 327712 | tf_op jit(solution)/shard_map/all_to_all | solution.py:287
  61.8 0.1 copy.10
  61.9 0.0 collective-permute-done.3.refs_3_
  61.9 0.0 collective-permute-done.2.refs_2_
  61.9 0.0 collective-permute-done.1.refs_1_
  61.9 0.0 copy-done
  61.9 2.2 %contract.1 = bf16[13,128,128]{2,1,0:T(8,128)(2,1)S(1)} custom-call(s32[1]{0:T(128)} %bitcast.me_ref, bf16[20,64,128]{2,1,0:T(8,128)(2,1)S(1)} %bitcast.9, bf16[3760,128]{1,0:T(8,128)(2,1)S(1)} %copy-done, bf16[3760,128]{1,0:T(8,128)(2,1)} %collective-permute-done.1.refs_1_, bf16[3760,128]{1,0:T(8,128)(2,1)S(1)} %collective-permute-done.2.refs_2_, ...), custom_call_target="tpu_custom_call" | custom-call | tf_op jit(solution)/shard_map/contract/pallas_call | solution.py:223
  64.1 0.3 copy.7
  64.4 28.1 %all_to_all.15 = bf16[13,128,128]{2,0,1:T(8,128)(2,1)S(1)} all-to-all(bf16[13,128,128]{2,0,1:T(8,128)(2,1)S(1)} %copy.7), channel_id=1, replica_groups=mesh['y4'=2,'y2'=2,'y1'=2,'z4'=2,'z2'=2,'z1'=2,'core'=2,'pair'=4] {'core..., dimensions={1} | all-to-all | bytes 851968 | tf_op jit(solution)/shard_map/all_to_all | solution.py:289
  92.5 0.1 copy.8.r_ref
  92.6 1.2 %place_rows.1 = bf16[1600,128]{1,0:T(8,128)(2,1)} custom-call(bf16[13,128,128]{2,1,0:T(8,128)(2,1)S(1)} %copy.8.r_ref), custom_call_target="tpu_custom_call" | custom-call | tf_op jit(solution)/shard_map/place_rows/pallas_call | solution.py:260
Async XLA Ops:
  0.0 29.3 %copy-start.1 = (bf16[48,1,800]{2,0,1:T(8,128)(2,1)S(1)}, bf16[48,1,800]{2,0,1:T(8,128)(2,1)}, u32[]{:S(2)}) copy-start(bf16[48,1,800]{2,0,1:T(8,128)(2,1)} %param.4) | copy-start | bytes 230404
  3.2 58.7 %collective-permute-start.3 = (bf16[3760,128]{1,0:T(8,128)(2,1)}, bf16[3760,128]{1,0:T(8,128)(2,1)S(1)}, u32[]{:S(2)}, u32[]{:S(2)}) collective-permute-start(bf16[3760,128]{1,0:T(8,128)(2,1)} %get-tuple-element.8.refs_0_), channel_id=1, source_target_pairs={{3,0},{2,1},{1,2},{0,3},{7,4},{6,5},{5,6},{4,7},{11,8},{10,9},{9,1... | collective-permute-start | bytes 2887688 | tf_op jit(solution)/shard_map/ppermute | solution.py:284
  8.4 53.5 %collective-permute-start.2 = (bf16[3760,128]{1,0:T(8,128)(2,1)}, bf16[3760,128]{1,0:T(8,128)(2,1)S(1)}, u32[]{:S(2)}, u32[]{:S(2)}) collective-permute-start(bf16[3760,128]{1,0:T(8,128)(2,1)} %get-tuple-element.8.refs_0_), channel_id=1, source_target_pairs={{2,0},{3,1},{0,2},{1,3},{6,4},{7,5},{4,6},{5,7},{10,8},{11,9},{8,1... | collective-permute-start | bytes 2887688 | tf_op jit(solution)/shard_map/ppermute | solution.py:284
  10.8 51.1 %collective-permute-start.1 = (bf16[3760,128]{1,0:T(8,128)(2,1)}, bf16[3760,128]{1,0:T(8,128)(2,1)}, u32[]{:S(2)}, u32[]{:S(2)}) collective-permute-start(bf16[3760,128]{1,0:T(8,128)(2,1)} %get-tuple-element.8.refs_0_), channel_id=1, source_target_pairs={{1,0},{0,1},{3,2},{2,3},{5,4},{4,5},{7,6},{6,7},{9,8},{8,9},{11,10... | collective-permute-start | bytes 2887688 | tf_op jit(solution)/shard_map/ppermute | solution.py:284
  12.8 28.0 %all-to-all-start = ((bf16[64,8,128]{2,1,0:T(8,128)(2,1)}), bf16[64,8,128]{2,1,0:T(8,128)(2,1)S(1)}, u32[]{:S(2)}, u32[]{:S(2)}) async-start(bf16[64,8,128]{2,1,0:T(8,128)(2,1)} %get-tuple-element.7), calls=%async_computation | async-start | bytes 262144 | tf_op jit(solution)/shard_map/all_to_all | solution.py:279
  29.3 4.6 %collective-permute-start = (bf16[48,800]{1,0:T(8,128)(2,1)S(1)}, bf16[48,800]{1,0:T(8,128)(2,1)S(1)}, u32[]{:S(2)}, u32[]{:S(2)}) collective-permute-start(bf16[48,800]{1,0:T(8,128)(2,1)S(1)} %bitcast.10), channel_id=1, source_target_pairs={{0,4},{4,0},{1,5},{5,1},{2,6},{6,2},{3,7},{7,3},{8,12},{12,8},{9,1... | collective-permute-start | bytes 230408 | tf_op jit(solution)/shard_map/ppermute | solution.py:281
  34.0 27.9 %copy-start = (bf16[3760,128]{1,0:T(8,128)(2,1)S(1)}, bf16[3760,128]{1,0:T(8,128)(2,1)}, u32[]{:S(2)}) copy-start(bf16[3760,128]{1,0:T(8,128)(2,1)} %get-tuple-element.8.refs_0_) | copy-start | bytes 2887684
  42.4 19.4 %all-to-all-start.1 = ((bf16[64,20,128]{2,1,0:T(8,128)(2,1)}), bf16[64,20,128]{2,1,0:T(8,128)(2,1)S(1)}, u32[]{:S(2)}, u32[]{:S(2)}) async-start(bf16[64,20,128]{2,1,0:T(8,128)(2,1)} %select_pieces.1), calls=%async_computation.1 | async-start | bytes 786432 | tf_op jit(solution)/shard_map/all_to_all | solution.py:287

commit v5 on v4

--- a/solution.py
+++ b/solution.py
@@ -194,17 +194,18 @@
     )(table, asked)
 
 
-def contract_kernel(depth, columns, me_ref, a_ref, *refs):
-    parts, out_ref, tails = refs[:-2], refs[-2], refs[-1]
-    ring = len(parts)
+def contract_kernel(depth, columns, steps, me_ref, a_ref, *refs):
+    parts, earlier, out_ref, tails = refs[: len(steps)], refs[len(steps) : -2], refs[-2], refs[-1]
     chunks = a_ref.shape[0] // 2
     slabs = columns // LANES
     left = columns - slabs * LANES
     halves = [jnp.concatenate([a_ref[r * chunks + j] for j in range(chunks)], axis=1) for r in range(2)]
     a = jnp.concatenate(halves, axis=0)
     tails[...] = jnp.zeros_like(tails)
-    for step, part in enumerate(parts):
-        p = jnp.bitwise_xor(me_ref[0], PLACES[step])
+    for before in earlier:
+        out_ref[...] = before[...]
+    for step, part in zip(steps, parts):
+        p = jnp.bitwise_xor(me_ref[0], step)
         wide = jnp.concatenate([part[s * depth : (s + 1) * depth, :] for s in range(slabs)], axis=1)
         product = jnp.dot(a[:, :depth], wide, preferred_element_type=F32).astype(BF16)
         for s in range(slabs):
@@ -212,23 +213,24 @@
         narrow = [part[at : at + left, :] for at in range(slabs * depth, part.shape[0], left)]
         tails[pl.ds(pl.multiple_of(p * left, left), left), :] = jnp.concatenate(narrow, axis=1)
     last = lax.dot_general(a, tails[...], (((1,), (1,)), ((), ())), preferred_element_type=F32)
+    for before in earlier:
+        last = last + before[before.shape[0] - 1].astype(F32)
     out_ref[out_ref.shape[0] - 1] = last.astype(BF16)
 
 
-def contract(depth, columns, me, arrived, parts):
-    ring = len(parts)
+def contract(depth, columns, ring, me, arrived, steps, parts, earlier=()):
     chunks2, peers, _ = arrived.shape
     outs = ring * (columns // LANES) + 1
     whole = pl.BlockSpec(memory_space=pltpu.VMEM)
     return pl.pallas_call(
-        functools.partial(contract_kernel, depth, columns),
+        functools.partial(contract_kernel, depth, columns, steps),
         out_shape=jax.ShapeDtypeStruct((outs, 2 * peers, LANES), BF16),
-        in_specs=[pl.BlockSpec(memory_space=pltpu.SMEM)] + [whole] * (1 + ring),
+        in_specs=[pl.BlockSpec(memory_space=pltpu.SMEM)] + [whole] * (1 + len(parts) + len(earlier)),
         out_specs=whole,
         scratch_shapes=[pltpu.VMEM((LANES, chunks2 // 2 * LANES), BF16)],
         compiler_params=pltpu.CompilerParams(vmem_limit_bytes=24 << 20),
         name="contract",
-    )(me, arrived, *parts)
+    )(me, arrived, *parts, *earlier)
 
 
 def place_kernel(columns, sizes, r_ref, out_ref):
@@ -285,7 +287,9 @@
 
     outgoing = select(slots, table, asked)
     arrived = jnp.transpose(lax.all_to_all(outgoing, SERVED, 0, 0, tiled=True), (1, 0, 2))
-    rows = contract(depth, columns, lax.axis_index("pair").reshape(1), arrived, parts)
+    here = lax.axis_index("pair").reshape(1)
+    rows = contract(depth, columns, ring, here, arrived, (PLACES[0], PLACES[3]), [parts[0], parts[3]])
+    rows = contract(depth, columns, ring, here, arrived, PLACES[1:3], parts[1:3], (rows,))
     received = lax.all_to_all(rows, ("core", *SERVED), 1, 1, tiled=True)
     return place(columns, sizes, received).T[None]
 

time: 94.3 us -> 94.6 us (level)
    pallas_call x1 -> x2, Pallas kernels: 2.16 us -> 2.43 us  [contract(): pl.pallas_call(functools.partial(contract_kernel, depth, columns, steps),...]
  transfers between devices with their start and end apart: 6 -> 6, of which waited for: 3 -> 3; matrix products, arithmetic and copies ran while one was open for 0% -> 0% of each run, Pallas kernels for 2% -> 4%
where the time goes in v5:
time: 94.6 us; the launch traced here: 94.2 us
  starting transfers between devices  35.5 us (38%)
  blocking collectives  28.1 us (30%)
  waiting for transfers between devices  21.3 us (23%)
  Pallas kernels  7.92 us (8%)
    all_to_all x1, blocking collectives, local(): received = lax.all_to_all(rows, ('core', *SERVED), 1, 1, tiled=True)  28.1 us
    all_to_all x1, starting transfers between devices, local(): asked = lax.all_to_all(wanted, SERVED, 0, 0, tiled=True)  16.5 us
    all_to_all x1, waiting for transfers between devices, local(): lax.all_to_all(outgoing, SERVED, 0, 0, tiled=True)  13.7 us
    ppermute x3, starting transfers between devices, local(): lax.ppermute(packed, 'pair', [(i ^ k, i) for i in range(ring)])  9.62 us
    all_to_all x1, waiting for transfers between devices, local(): asked = lax.all_to_all(wanted, SERVED, 0, 0, tiled=True)  6.68 us
    all_to_all x1, starting transfers between devices, local(): lax.all_to_all(outgoing, SERVED, 0, 0, tiled=True)  5.64 us
    ppermute x1, starting transfers between devices, local(): other = lax.ppermute(own, 'core', [(0, 1), (1, 0)])  3.7 us
    pallas_call x1, Pallas kernels, pack(): pl.pallas_call(functools.partial(pack_kernel, window), out_shape=[jax.Sha...  2.48 us
  transfers between devices with their start and end apart: 6, of which 3 were waited for; matrix products, arithmetic and copies ran while one was open for 0% of the time, Pallas kernels for 4%

profile of v5, /device:TPU:1, one launch (start us, length us, event | category | flops | bytes accessed | tf_op | source)
XLA Modules:
  0.0 94.2 jit_solution(8823273644010349253)
XLA Ops:
  0.0 0.0 copy-start.1
  0.7 2.5 %pack_integrals.1 = (bf16[3760,128]{1,0:T(8,128)(2,1)}, bf16[64,8,128]{2,1,0:T(8,128)(2,1)}) custom-call(bf16[6,200,400]{2,1,0:T(8,128)(2,1)} %w_hbm.1, s32[6]{0:T(128)} %column_hbm.1, s32[1]{0:T(128)S(6)} %copy.11.symmetry_hbm), custom_call_target="tpu_custom_call" | custom-call | tf_op jit(solution)/shard_map/pack_integrals/pallas_call | solution.py:99
  3.2 5.2 %collective-permute-start.3 = (bf16[3760,128]{1,0:T(8,128)(2,1)}, bf16[3760,128]{1,0:T(8,128)(2,1)}, u32[]{:S(2)}, u32[]{:S(2)}) collective-permute-start(bf16[3760,128]{1,0:T(8,128)(2,1)} %get-tuple-element.8.refs_0_), channel_id=1, source_target_pairs={{3,0},{2,1},{1,2},{0,3},{7,4},{6,5},{5,6},{4,7},{11,8},{10,9},{9,1... | collective-permute-start | bytes 2887688 | tf_op jit(solution)/shard_map/ppermute | solution.py:286
  8.4 2.4 %collective-permute-start.2 = (bf16[3760,128]{1,0:T(8,128)(2,1)}, bf16[3760,128]{1,0:T(8,128)(2,1)S(1)}, u32[]{:S(2)}, u32[]{:S(2)}) collective-permute-start(bf16[3760,128]{1,0:T(8,128)(2,1)} %get-tuple-element.8.refs_0_), channel_id=1, source_target_pairs={{2,0},{3,1},{0,2},{1,3},{6,4},{7,5},{4,6},{5,7},{10,8},{11,9},{8,1... | collective-permute-start | bytes 2887688 | tf_op jit(solution)/shard_map/ppermute | solution.py:286
  10.8 2.0 %collective-permute-start.1 = (bf16[3760,128]{1,0:T(8,128)(2,1)}, bf16[3760,128]{1,0:T(8,128)(2,1)S(1)}, u32[]{:S(2)}, u32[]{:S(2)}) collective-permute-start(bf16[3760,128]{1,0:T(8,128)(2,1)} %get-tuple-element.8.refs_0_), channel_id=1, source_target_pairs={{1,0},{0,1},{3,2},{2,3},{5,4},{4,5},{7,6},{6,7},{9,8},{8,9},{11,10... | collective-permute-start | bytes 2887688 | tf_op jit(solution)/shard_map/ppermute | solution.py:286
  12.8 16.5 %all-to-all-start = ((bf16[64,8,128]{2,1,0:T(8,128)(2,1)}), bf16[64,8,128]{2,1,0:T(8,128)(2,1)S(1)}, u32[]{:S(2)}, u32[]{:S(2)}) async-start(bf16[64,8,128]{2,1,0:T(8,128)(2,1)} %get-tuple-element.7), calls=%async_computation | async-start | bytes 262144 | tf_op jit(solution)/shard_map/all_to_all | solution.py:281
  29.3 0.0 copy-done.1
  29.3 3.7 %collective-permute-start = (bf16[48,800]{1,0:T(8,128)(2,1)S(1)}, bf16[48,800]{1,0:T(8,128)(2,1)S(1)}, u32[]{:S(2)}, u32[]{:S(2)}) collective-permute-start(bf16[48,800]{1,0:T(8,128)(2,1)S(1)} %bitcast.11), channel_id=1, source_target_pairs={{0,4},{4,0},{1,5},{5,1},{2,6},{6,2},{3,7},{7,3},{8,12},{12,8},{9,1... | collective-permute-start | bytes 230408 | tf_op jit(solution)/shard_map/ppermute | solution.py:283
  33.1 0.9 collective-permute-done.other_ref
  34.0 0.0 copy-start
  34.0 0.1 build_table.1.table_ref
  34.1 6.7 %all-to-all-done.asked_ref = bf16[64,8,128]{2,1,0:T(8,128)(2,1)S(1)} async-done(((bf16[64,8,128]{2,1,0:T(8,128)(2,1)}), bf16[64,8,128]{2,1,0:T(8,128)(2,1)S(1)}, u32[]{:S(2)}, u32[]{:S(2)}) %all-to-all-start) | async-done | bytes 131104 | tf_op jit(solution)/shard_map/all_to_all | solution.py:281
  40.8 1.7 %select_pieces.1 = bf16[64,20,128]{2,1,0:T(8,128)(2,1)} custom-call(bf16[192,512]{1,0:T(8,128)(2,1)S(1)} %build_table.1.table_ref, bf16[64,8,128]{2,1,0:T(8,128)(2,1)S(1)} %all-to-all-done.asked_ref), custom_call_target="tpu_custom_call" | custom-call | tf_op jit(solution)/shard_map/select_pieces/pallas_call | solution.py:182
  42.4 5.6 %all-to-all-start.1 = ((bf16[64,20,128]{2,1,0:T(8,128)(2,1)}), bf16[64,20,128]{2,1,0:T(8,128)(2,1)S(1)}, u32[]{:S(2)}, u32[]{:S(2)}) async-start(bf16[64,20,128]{2,1,0:T(8,128)(2,1)} %select_pieces.1), calls=%async_computation.1 | async-start | bytes 786432 | tf_op jit(solution)/shard_map/all_to_all | solution.py:289
  48.1 13.7 %all-to-all-done.1 = bf16[64,20,128]{2,1,0:T(8,128)(2,1)S(1)} async-done(((bf16[64,20,128]{2,1,0:T(8,128)(2,1)}), bf16[64,20,128]{2,1,0:T(8,128)(2,1)S(1)}, u32[]{:S(2)}, u32[]{:S(2)}) %all-to-all-start.1) | async-done | bytes 327712 | tf_op jit(solution)/shard_map/all_to_all | solution.py:289
  61.8 0.1 copy.10
  61.9 0.0 collective-permute-done.3.refs_1_
  61.9 0.0 copy-done
  61.9 1.8 %contract.2.refs_2_ = bf16[13,128,128]{2,1,0:T(8,128)(2,1)S(1)} custom-call(s32[1]{0:T(128)} %bitcast.me_ref, bf16[20,64,128]{2,1,0:T(8,128)(2,1)S(1)} %bitcast.9, bf16[3760,128]{1,0:T(8,128)(2,1)S(1)} %copy-done, bf16[3760,128]{1,0:T(8,128)(2,1)} %collective-permute-done.3.refs_1_), custom_call_target="tpu_custom_call" | custom-call | tf_op jit(solution)/shard_map/contract/pallas_call | solution.py:225
  63.7 0.0 collective-permute-done.2.refs_1_
  63.7 0.0 collective-permute-done.1.refs_0_
  63.7 0.6 contract.3
  64.4 0.3 copy.7
  64.7 28.1 %all_to_all.15 = bf16[13,128,128]{2,0,1:T(8,128)(2,1)S(1)} all-to-all(bf16[13,128,128]{2,0,1:T(8,128)(2,1)S(1)} %copy.7), channel_id=1, replica_groups=mesh['y4'=2,'y2'=2,'y1'=2,'z4'=2,'z2'=2,'z1'=2,'core'=2,'pair'=4] {'core..., dimensions={1} | all-to-all | bytes 851968 | tf_op jit(solution)/shard_map/all_to_all | solution.py:293
  92.8 0.1 copy.8.r_ref
  92.9 1.2 %place_rows.1 = bf16[1600,128]{1,0:T(8,128)(2,1)} custom-call(bf16[13,128,128]{2,1,0:T(8,128)(2,1)S(1)} %copy.8.r_ref), custom_call_target="tpu_custom_call" | custom-call | tf_op jit(solution)/shard_map/place_rows/pallas_call | solution.py:262
Async XLA Ops:
  0.0 29.3 %copy-start.1 = (bf16[48,1,800]{2,0,1:T(8,128)(2,1)S(1)}, bf16[48,1,800]{2,0,1:T(8,128)(2,1)}, u32[]{:S(2)}) copy-start(bf16[48,1,800]{2,0,1:T(8,128)(2,1)} %param.4) | copy-start | bytes 230404
  3.2 58.7 %collective-permute-start.3 = (bf16[3760,128]{1,0:T(8,128)(2,1)}, bf16[3760,128]{1,0:T(8,128)(2,1)}, u32[]{:S(2)}, u32[]{:S(2)}) collective-permute-start(bf16[3760,128]{1,0:T(8,128)(2,1)} %get-tuple-element.8.refs_0_), channel_id=1, source_target_pairs={{3,0},{2,1},{1,2},{0,3},{7,4},{6,5},{5,6},{4,7},{11,8},{10,9},{9,1... | collective-permute-start | bytes 2887688 | tf_op jit(solution)/shard_map/ppermute | solution.py:286
  8.4 55.3 %collective-permute-start.2 = (bf16[3760,128]{1,0:T(8,128)(2,1)}, bf16[3760,128]{1,0:T(8,128)(2,1)S(1)}, u32[]{:S(2)}, u32[]{:S(2)}) collective-permute-start(bf16[3760,128]{1,0:T(8,128)(2,1)} %get-tuple-element.8.refs_0_), channel_id=1, source_target_pairs={{2,0},{3,1},{0,2},{1,3},{6,4},{7,5},{4,6},{5,7},{10,8},{11,9},{8,1... | collective-permute-start | bytes 2887688 | tf_op jit(solution)/shard_map/ppermute | solution.py:286
  10.8 52.9 %collective-permute-start.1 = (bf16[3760,128]{1,0:T(8,128)(2,1)}, bf16[3760,128]{1,0:T(8,128)(2,1)S(1)}, u32[]{:S(2)}, u32[]{:S(2)}) collective-permute-start(bf16[3760,128]{1,0:T(8,128)(2,1)} %get-tuple-element.8.refs_0_), channel_id=1, source_target_pairs={{1,0},{0,1},{3,2},{2,3},{5,4},{4,5},{7,6},{6,7},{9,8},{8,9},{11,10... | collective-permute-start | bytes 2887688 | tf_op jit(solution)/shard_map/ppermute | solution.py:286
  12.8 28.0 %all-to-all-start = ((bf16[64,8,128]{2,1,0:T(8,128)(2,1)}), bf16[64,8,128]{2,1,0:T(8,128)(2,1)S(1)}, u32[]{:S(2)}, u32[]{:S(2)}) async-start(bf16[64,8,128]{2,1,0:T(8,128)(2,1)} %get-tuple-element.7), calls=%async_computation | async-start | bytes 262144 | tf_op jit(solution)/shard_map/all_to_all | solution.py:281
  29.3 4.6 %collective-permute-start = (bf16[48,800]{1,0:T(8,128)(2,1)S(1)}, bf16[48,800]{1,0:T(8,128)(2,1)S(1)}, u32[]{:S(2)}, u32[]{:S(2)}) collective-permute-start(bf16[48,800]{1,0:T(8,128)(2,1)S(1)} %bitcast.11), channel_id=1, source_target_pairs={{0,4},{4,0},{1,5},{5,1},{2,6},{6,2},{3,7},{7,3},{8,12},{12,8},{9,1... | collective-permute-start | bytes 230408 | tf_op jit(solution)/shard_map/ppermute | solution.py:283
  34.0 27.9 %copy-start = (bf16[3760,128]{1,0:T(8,128)(2,1)S(1)}, bf16[3760,128]{1,0:T(8,128)(2,1)}, u32[]{:S(2)}) copy-start(bf16[3760,128]{1,0:T(8,128)(2,1)} %get-tuple-element.8.refs_0_) | copy-start | bytes 2887684
  42.4 19.4 %all-to-all-start.1 = ((bf16[64,20,128]{2,1,0:T(8,128)(2,1)}), bf16[64,20,128]{2,1,0:T(8,128)(2,1)S(1)}, u32[]{:S(2)}, u32[]{:S(2)}) async-start(bf16[64,20,128]{2,1,0:T(8,128)(2,1)} %select_pieces.1), calls=%async_computation.1 | async-start | bytes 786432 | tf_op jit(solution)/shard_map/all_to_all | solution.py:289

commit v6 on v4

--- a/solution.py
+++ b/solution.py
@@ -100,7 +100,7 @@
         functools.partial(pack_kernel, window),
         out_shape=[
             jax.ShapeDtypeStruct((rows, LANES), BF16),
-            jax.ShapeDtypeStruct((peers, 8, LANES), BF16),
+            jax.ShapeDtypeStruct((peers, 4, LANES), BF16),
         ],
         in_specs=[anywhere, anywhere, anywhere],
         out_specs=[anywhere, anywhere],
@@ -109,7 +109,7 @@
             pltpu.SMEM(tile_column.shape, jnp.int32),
             pltpu.SMEM(block_symmetry.shape, jnp.int32),
             pltpu.VMEM((rows, LANES), BF16),
-            pltpu.VMEM((peers, 8, LANES), BF16),
+            pltpu.VMEM((peers, 4, LANES), BF16),
             pltpu.SemaphoreType.DMA((slots + 2,)),
             pltpu.SemaphoreType.DMA((slabs + 2,)),
         ],

time: 94.3 us -> 94.4 us (level)
  no operation moved by 1% of the time
where the time goes in v6:
time: 94.4 us; the launch traced here: 94 us
  starting transfers between devices  36 us (38%)
  blocking collectives  27.5 us (29%)
  waiting for transfers between devices  21.5 us (23%)
  Pallas kernels  7.67 us (8%)
    all_to_all x1, blocking collectives, local(): received = lax.all_to_all(rows, ('core', *SERVED), 1, 1, tiled=True)  27.5 us
    all_to_all x1, starting transfers between devices, local(): asked = lax.all_to_all(wanted, SERVED, 0, 0, tiled=True)  16.5 us
    all_to_all x1, waiting for transfers between devices, local(): lax.all_to_all(outgoing, SERVED, 0, 0, tiled=True)  14.4 us
    ppermute x3, starting transfers between devices, local(): lax.ppermute(packed, 'pair', [(i ^ k, i) for i in range(ring)])  9.62 us
    all_to_all x1, waiting for transfers between devices, local(): asked = lax.all_to_all(wanted, SERVED, 0, 0, tiled=True)  6.2 us
    all_to_all x1, starting transfers between devices, local(): lax.all_to_all(outgoing, SERVED, 0, 0, tiled=True)  6.12 us
    ppermute x1, starting transfers between devices, local(): other = lax.ppermute(own, 'core', [(0, 1), (1, 0)])  3.7 us
    pallas_call x1, Pallas kernels, pack(): pl.pallas_call(functools.partial(pack_kernel, window), out_shape=[jax.Sha...  2.48 us
  transfers between devices with their start and end apart: 6, of which 3 were waited for; matrix products, arithmetic and copies ran while one was open for 0% of the time, Pallas kernels for 2%

profile of v6, /device:TPU:1, one launch (start us, length us, event | category | flops | bytes accessed | tf_op | source)
XLA Modules:
  0.0 94.0 jit_solution(1251228169229221276)
XLA Ops:
  0.0 0.0 copy-start.1
  0.7 2.5 %pack_integrals.1 = (bf16[3760,128]{1,0:T(8,128)(2,1)}, bf16[64,4,128]{2,1,0:T(4,128)(2,1)}) custom-call(bf16[6,200,400]{2,1,0:T(8,128)(2,1)} %w_hbm.1, s32[6]{0:T(128)} %column_hbm.1, s32[1]{0:T(128)S(6)} %copy.11.symmetry_hbm), custom_call_target="tpu_custom_call" | custom-call | tf_op jit(solution)/shard_map/pack_integrals/pallas_call | solution.py:99
  3.2 5.2 %collective-permute-start.3 = (bf16[3760,128]{1,0:T(8,128)(2,1)}, bf16[3760,128]{1,0:T(8,128)(2,1)S(1)}, u32[]{:S(2)}, u32[]{:S(2)}) collective-permute-start(bf16[3760,128]{1,0:T(8,128)(2,1)} %get-tuple-element.8.refs_0_), channel_id=1, source_target_pairs={{3,0},{2,1},{1,2},{0,3},{7,4},{6,5},{5,6},{4,7},{11,8},{10,9},{9,1... | collective-permute-start | bytes 2887688 | tf_op jit(solution)/shard_map/ppermute | solution.py:284
  8.4 2.4 %collective-permute-start.2 = (bf16[3760,128]{1,0:T(8,128)(2,1)}, bf16[3760,128]{1,0:T(8,128)(2,1)S(1)}, u32[]{:S(2)}, u32[]{:S(2)}) collective-permute-start(bf16[3760,128]{1,0:T(8,128)(2,1)} %get-tuple-element.8.refs_0_), channel_id=1, source_target_pairs={{2,0},{3,1},{0,2},{1,3},{6,4},{7,5},{4,6},{5,7},{10,8},{11,9},{8,1... | collective-permute-start | bytes 2887688 | tf_op jit(solution)/shard_map/ppermute | solution.py:284
  10.8 2.0 %collective-permute-start.1 = (bf16[3760,128]{1,0:T(8,128)(2,1)}, bf16[3760,128]{1,0:T(8,128)(2,1)}, u32[]{:S(2)}, u32[]{:S(2)}) collective-permute-start(bf16[3760,128]{1,0:T(8,128)(2,1)} %get-tuple-element.8.refs_0_), channel_id=1, source_target_pairs={{1,0},{0,1},{3,2},{2,3},{5,4},{4,5},{7,6},{6,7},{9,8},{8,9},{11,10... | collective-permute-start | bytes 2887688 | tf_op jit(solution)/shard_map/ppermute | solution.py:284
  12.8 16.5 %all-to-all-start = ((bf16[64,4,128]{2,1,0:T(4,128)(2,1)}), bf16[64,4,128]{2,1,0:T(4,128)(2,1)S(1)}, u32[]{:S(2)}, u32[]{:S(2)}) async-start(bf16[64,4,128]{2,1,0:T(4,128)(2,1)} %get-tuple-element.7), calls=%async_computation | async-start | bytes 131072 | tf_op jit(solution)/shard_map/all_to_all | solution.py:279
  29.3 0.0 copy-done.1
  29.3 3.7 %collective-permute-start = (bf16[48,800]{1,0:T(8,128)(2,1)S(1)}, bf16[48,800]{1,0:T(8,128)(2,1)S(1)}, u32[]{:S(2)}, u32[]{:S(2)}) collective-permute-start(bf16[48,800]{1,0:T(8,128)(2,1)S(1)} %bitcast.10), channel_id=1, source_target_pairs={{0,4},{4,0},{1,5},{5,1},{2,6},{6,2},{3,7},{7,3},{8,12},{12,8},{9,1... | collective-permute-start | bytes 230408 | tf_op jit(solution)/shard_map/ppermute | solution.py:281
  33.1 0.9 collective-permute-done.other_ref
  34.0 0.0 copy-start
  34.0 0.1 build_table.1.table_ref
  34.1 6.2 %all-to-all-done.asked_ref = bf16[64,4,128]{2,1,0:T(4,128)(2,1)S(1)} async-done(((bf16[64,4,128]{2,1,0:T(4,128)(2,1)}), bf16[64,4,128]{2,1,0:T(4,128)(2,1)S(1)}, u32[]{:S(2)}, u32[]{:S(2)}) %all-to-all-start) | async-done | bytes 65568 | tf_op jit(solution)/shard_map/all_to_all | solution.py:279
  40.3 1.7 %select_pieces.1 = bf16[64,20,128]{2,1,0:T(8,128)(2,1)} custom-call(bf16[192,512]{1,0:T(8,128)(2,1)S(1)} %build_table.1.table_ref, bf16[64,4,128]{2,1,0:T(4,128)(2,1)S(1)} %all-to-all-done.asked_ref), custom_call_target="tpu_custom_call" | custom-call | tf_op jit(solution)/shard_map/select_pieces/pallas_call | solution.py:182
  42.0 6.1 %all-to-all-start.1 = ((bf16[64,20,128]{2,1,0:T(8,128)(2,1)}), bf16[64,20,128]{2,1,0:T(8,128)(2,1)S(1)}, u32[]{:S(2)}, u32[]{:S(2)}) async-start(bf16[64,20,128]{2,1,0:T(8,128)(2,1)} %select_pieces.1), calls=%async_computation.1 | async-start | bytes 786432 | tf_op jit(solution)/shard_map/all_to_all | solution.py:287
  48.1 14.4 %all-to-all-done.1 = bf16[64,20,128]{2,1,0:T(8,128)(2,1)S(1)} async-done(((bf16[64,20,128]{2,1,0:T(8,128)(2,1)}), bf16[64,20,128]{2,1,0:T(8,128)(2,1)S(1)}, u32[]{:S(2)}, u32[]{:S(2)}) %all-to-all-start.1) | async-done | bytes 327712 | tf_op jit(solution)/shard_map/all_to_all | solution.py:287
  62.5 0.1 copy.10
  62.6 0.0 collective-permute-done.3.refs_3_
  62.6 0.0 collective-permute-done.2.refs_2_
  62.6 0.0 collective-permute-done.1.refs_1_
  62.6 0.0 copy-done
  62.6 2.2 %contract.1 = bf16[13,128,128]{2,1,0:T(8,128)(2,1)S(1)} custom-call(s32[1]{0:T(128)} %bitcast.me_ref, bf16[20,64,128]{2,1,0:T(8,128)(2,1)S(1)} %bitcast.9, bf16[3760,128]{1,0:T(8,128)(2,1)S(1)} %copy-done, bf16[3760,128]{1,0:T(8,128)(2,1)} %collective-permute-done.1.refs_1_, bf16[3760,128]{1,0:T(8,128)(2,1)S(1)} %collective-permute-done.2.refs_2_, ...), custom_call_target="tpu_custom_call" | custom-call | tf_op jit(solution)/shard_map/contract/pallas_call | solution.py:223
  64.8 0.3 copy.7
  65.1 27.5 %all_to_all.15 = bf16[13,128,128]{2,0,1:T(8,128)(2,1)S(1)} all-to-all(bf16[13,128,128]{2,0,1:T(8,128)(2,1)S(1)} %copy.7), channel_id=1, replica_groups=mesh['y4'=2,'y2'=2,'y1'=2,'z4'=2,'z2'=2,'z1'=2,'core'=2,'pair'=4] {'core..., dimensions={1} | all-to-all | bytes 851968 | tf_op jit(solution)/shard_map/all_to_all | solution.py:289
  92.6 0.1 copy.8.r_ref
  92.8 1.2 %place_rows.1 = bf16[1600,128]{1,0:T(8,128)(2,1)} custom-call(bf16[13,128,128]{2,1,0:T(8,128)(2,1)S(1)} %copy.8.r_ref), custom_call_target="tpu_custom_call" | custom-call | tf_op jit(solution)/shard_map/place_rows/pallas_call | solution.py:260
Async XLA Ops:
  0.0 29.3 %copy-start.1 = (bf16[48,1,800]{2,0,1:T(8,128)(2,1)S(1)}, bf16[48,1,800]{2,0,1:T(8,128)(2,1)}, u32[]{:S(2)}) copy-start(bf16[48,1,800]{2,0,1:T(8,128)(2,1)} %param.4) | copy-start | bytes 230404
  3.2 59.4 %collective-permute-start.3 = (bf16[3760,128]{1,0:T(8,128)(2,1)}, bf16[3760,128]{1,0:T(8,128)(2,1)S(1)}, u32[]{:S(2)}, u32[]{:S(2)}) collective-permute-start(bf16[3760,128]{1,0:T(8,128)(2,1)} %get-tuple-element.8.refs_0_), channel_id=1, source_target_pairs={{3,0},{2,1},{1,2},{0,3},{7,4},{6,5},{5,6},{4,7},{11,8},{10,9},{9,1... | collective-permute-start | bytes 2887688 | tf_op jit(solution)/shard_map/ppermute | solution.py:284
  8.4 54.2 %collective-permute-start.2 = (bf16[3760,128]{1,0:T(8,128)(2,1)}, bf16[3760,128]{1,0:T(8,128)(2,1)S(1)}, u32[]{:S(2)}, u32[]{:S(2)}) collective-permute-start(bf16[3760,128]{1,0:T(8,128)(2,1)} %get-tuple-element.8.refs_0_), channel_id=1, source_target_pairs={{2,0},{3,1},{0,2},{1,3},{6,4},{7,5},{4,6},{5,7},{10,8},{11,9},{8,1... | collective-permute-start | bytes 2887688 | tf_op jit(solution)/shard_map/ppermute | solution.py:284
  10.8 51.8 %collective-permute-start.1 = (bf16[3760,128]{1,0:T(8,128)(2,1)}, bf16[3760,128]{1,0:T(8,128)(2,1)}, u32[]{:S(2)}, u32[]{:S(2)}) collective-permute-start(bf16[3760,128]{1,0:T(8,128)(2,1)} %get-tuple-element.8.refs_0_), channel_id=1, source_target_pairs={{1,0},{0,1},{3,2},{2,3},{5,4},{4,5},{7,6},{6,7},{9,8},{8,9},{11,10... | collective-permute-start | bytes 2887688 | tf_op jit(solution)/shard_map/ppermute | solution.py:284
  12.8 27.5 %all-to-all-start = ((bf16[64,4,128]{2,1,0:T(4,128)(2,1)}), bf16[64,4,128]{2,1,0:T(4,128)(2,1)S(1)}, u32[]{:S(2)}, u32[]{:S(2)}) async-start(bf16[64,4,128]{2,1,0:T(4,128)(2,1)} %get-tuple-element.7), calls=%async_computation | async-start | bytes 131072 | tf_op jit(solution)/shard_map/all_to_all | solution.py:279
  29.3 4.6 %collective-permute-start = (bf16[48,800]{1,0:T(8,128)(2,1)S(1)}, bf16[48,800]{1,0:T(8,128)(2,1)S(1)}, u32[]{:S(2)}, u32[]{:S(2)}) collective-permute-start(bf16[48,800]{1,0:T(8,128)(2,1)S(1)} %bitcast.10), channel_id=1, source_target_pairs={{0,4},{4,0},{1,5},{5,1},{2,6},{6,2},{3,7},{7,3},{8,12},{12,8},{9,1... | collective-permute-start | bytes 230408 | tf_op jit(solution)/shard_map/ppermute | solution.py:281
  34.0 28.7 %copy-start = (bf16[3760,128]{1,0:T(8,128)(2,1)S(1)}, bf16[3760,128]{1,0:T(8,128)(2,1)}, u32[]{:S(2)}) copy-start(bf16[3760,128]{1,0:T(8,128)(2,1)} %get-tuple-element.8.refs_0_) | copy-start | bytes 2887684
  42.0 20.5 %all-to-all-start.1 = ((bf16[64,20,128]{2,1,0:T(8,128)(2,1)}), bf16[64,20,128]{2,1,0:T(8,128)(2,1)S(1)}, u32[]{:S(2)}, u32[]{:S(2)}) async-start(bf16[64,20,128]{2,1,0:T(8,128)(2,1)} %select_pieces.1), calls=%async_computation.1 | async-start | bytes 786432 | tf_op jit(solution)/shard_map/all_to_all | solution.py:287
